TPU v7x, 32 devices: a whole 2x2x4 slice. The times are simulated.
32 devices in a mesh: fsdp: 8 (over z, x), seq: 4 (over y, core).
Axes of the slice: x: 2, y: 2, z: 4, core: 2. Of those that a mesh axis runs over, the one named last changes fastest.
Arguments:
- frames_in: bfloat16 [8, 1024, 768], P('fsdp', 'seq'), may hold values from -6 to 6
- norm1_gain: bfloat16 [768], P('fsdp'), may hold values from 0.099609375 to 1.8984375
- norm1_bias: bfloat16 [768], P('fsdp'), may hold values from -1.75 to 1.75
- qkv_weight: bfloat16 [768, 2304], P('fsdp'), may hold values from -0.21875 to 0.21875
- query_bias: bfloat16 [768], P('fsdp'), may hold values from -3 to 3
- value_bias: bfloat16 [768], P('fsdp'), may hold values from -1.75 to 1.75
- out_weight: bfloat16 [768, 768], P('fsdp'), may hold values from -3 to 3
- out_bias: bfloat16 [768], P('fsdp'), may hold values from -1.75 to 1.75
- norm2_gain: bfloat16 [768], P('fsdp'), may hold values from 0.099609375 to 1.8984375
- norm2_bias: bfloat16 [768], P('fsdp'), may hold values from -1.75 to 1.75
- up_weight: bfloat16 [768, 3072], P('fsdp'), may hold values from -0.21875 to 0.21875
- up_bias: bfloat16 [3072], P('fsdp'), may hold values from -3 to 3
- down_weight: bfloat16 [3072, 768], P('fsdp'), may hold values from -0.109375 to 0.109375
- down_bias: bfloat16 [768], P('fsdp'), may hold values from -1.75 to 1.75
- cotangent: bfloat16 [8, 1024, 768], P('fsdp', 'seq'), may hold values from -6 to 6
Outputs:
- layer_out: bfloat16 [8, 1024, 768], P('fsdp', 'seq')
- input_grad: bfloat16 [8, 1024, 768], P('fsdp', 'seq')
- norm1_gain_grad: float32 [768], P('fsdp')
- norm1_bias_grad: float32 [768], P('fsdp')
- qkv_weight_grad: float32 [768, 2304], P('fsdp', 'seq')
- query_bias_grad: float32 [768], P('fsdp')
- value_bias_grad: float32 [768], P('fsdp')
- out_weight_grad: float32 [768, 768], P('fsdp', 'seq')
- out_bias_grad: float32 [768], P('fsdp')
- norm2_gain_grad: float32 [768], P('fsdp')
- norm2_bias_grad: float32 [768], P('fsdp')
- up_weight_grad: float32 [768, 3072], P('fsdp', 'seq')
- up_bias_grad: float32 [3072], P('fsdp')
- down_weight_grad: float32 [3072, 768], P('fsdp', 'seq')
- down_bias_grad: float32 [768], P('fsdp')
All inputs are finite; a program needn't handle non-finite values.
Results may differ from a plain program's by a relative error of at most 0.012.
Values may be sent and summed in bfloat16 or wider, within the bound.
No kernel may reach another device: no remote copies, remote signals or barrier semaphores. Data moves between devices by JAX's collectives and lax.ppermute only.
A program may use at most 128 MiB of HBM per device.

v0:
```python
import functools

import jax
import jax.numpy as jnp
from jax import lax
from jax.experimental import pallas as pl
from jax.experimental.pallas import tpu as pltpu
from jax.sharding import PartitionSpec as P

HD = 64
GROUPS = 4
epsilon = 1e-05
BF = jnp.bfloat16
F32 = jnp.float32


def dot(a, b):
    return jnp.dot(a, b, preferred_element_type=F32)


def dot_tn(a, b):
    return lax.dot_general(a, b, (((0,), (0,)), ((), ())), preferred_element_type=F32)


def dot_nt(a, b):
    return lax.dot_general(a, b, (((1,), (1,)), ((), ())), preferred_element_type=F32)


def seq_swap(value, step):
    return lax.ppermute(value, "seq", [(i, i ^ step) for i in range(GROUPS)])


def seq_pieces(value):
    near = seq_swap(value, 1)
    far = seq_swap(value, 2)
    return [value, near, far, seq_swap(far, 1)]


def fsdp_reduce(blocks):
    return lax.psum_scatter(blocks, "fsdp", scatter_dimension=0, tiled=False)


def side_swap(value, count):
    return lax.ppermute(value, "fsdp", [(i, i ^ 1) for i in range(count)])


def plane_swaps(parts, count):
    return [
        lax.ppermute(part, "fsdp", [(i, i ^ (2 * step)) for i in range(count)])
        for step, part in enumerate(parts, 1)
    ]


def add_all(own, arrived):
    for part in arrived:
        own = own + part.astype(F32)
    return own


def ring_order(count):
    return list(range(0, count, 2)) + list(range(count - 1, 0, -2))


def ring_gather(value, count):
    order = ring_order(count)
    ahead = [(order[i], order[(i + 1) % count]) for i in range(count)]
    back = [(b, a) for a, b in ahead]
    half = value.shape[0] // 32 * 16
    blocks, shifts = [value], [0]
    left = right = value
    for step in range(1, count // 2):
        left = lax.ppermute(left, "fsdp", ahead)
        right = lax.ppermute(right, "fsdp", back)
        blocks += [left, right]
        shifts += [-step, step]
    last = [lax.ppermute(left[:half], "fsdp", ahead), lax.ppermute(right[half:], "fsdp", back)]
    blocks.append(jnp.concatenate(last, 0))
    shifts.append(count // 2)
    spot = jnp.array([order.index(i) for i in range(count)], jnp.int32)[lax.axis_index("fsdp")]
    sources = jnp.array(order, jnp.int32)[(spot + jnp.array(shifts, jnp.int32)) % count]
    return sources, blocks


def after(value, *others):
    return lax.optimization_barrier((value,) + others)[0]


def to_groups(value, count):
    q = count // GROUPS
    pairs = []
    for s in range(GROUPS):
        for j in range(q):
            for t in range(GROUPS):
                pairs.append(((q * s + j) * GROUPS + t, (GROUPS * j + t) * GROUPS + s))
    return lax.ppermute(value, ("fsdp", "seq"), pairs)


def to_owners(value, count, step):
    q = count // GROUPS
    pairs = []
    for s in range(GROUPS):
        for j in range(q):
            for t in range(GROUPS):
                pairs.append(
                    ((GROUPS * j + t) * GROUPS + s, (q * s + j) * GROUPS + (t ^ step))
                )
    return lax.ppermute(value, ("fsdp", "seq"), pairs)


def normalise(values):
    center = values - jnp.mean(values, -1, keepdims=True)
    rstd = lax.rsqrt(jnp.mean(center * center, -1, keepdims=True) + epsilon)
    return center * rstd, rstd


def norm_back(grad, gain, xhat, rstd):
    e = grad * gain
    return rstd * (
        e - jnp.mean(e, -1, keepdims=True) - xhat * jnp.mean(e * xhat, -1, keepdims=True)
    )


def params(megabytes=26):
    return pltpu.CompilerParams(vmem_limit_bytes=megabytes * 2**20)


SMEM = pl.BlockSpec(memory_space=pltpu.SMEM)
VMEM = pl.BlockSpec(memory_space=pltpu.VMEM)
ANY = pl.BlockSpec(memory_space=pl.ANY)


def run(kernel, scalars, arrays, out_shape, scratch, megabytes, micros, direct=False):
    n_scalars, n_arrays, n_outs = len(scalars), len(arrays), len(out_shape)

    estimate = pl.CostEstimate(
        flops=int(micros * 10**9), bytes_accessed=2**20, transcendentals=0
    )
    if direct:
        return pl.pallas_call(
            kernel,
            out_shape=tuple(out_shape),
            in_specs=[SMEM] * n_scalars + [VMEM] * n_arrays,
            out_specs=(VMEM,) * n_outs,
            scratch_shapes=list(scratch),
            compiler_params=params(megabytes),
            cost_estimate=estimate,
        )(*scalars, *arrays)

    def wrapped(*refs):
        rest = refs[n_scalars + n_arrays :]
        outs, own = rest[:n_outs], rest[n_outs : n_outs + len(scratch)]
        held, sems = rest[n_outs + len(scratch) : -1], rest[-1]
        copies = [
            pltpu.make_async_copy(refs[n_scalars + i], held[i], sems.at[i])
            for i in range(n_arrays)
        ]
        for copy in copies:
            copy.start()
        for copy in copies:
            copy.wait()
        kernel(*refs[:n_scalars], *held, *outs, *own)

    return pl.pallas_call(
        wrapped,
        out_shape=tuple(out_shape),
        in_specs=[SMEM] * n_scalars + [ANY] * n_arrays,
        out_specs=(VMEM,) * n_outs,
        scratch_shapes=list(scratch)
        + [pltpu.VMEM(a.shape, a.dtype) for a in arrays]
        + [pltpu.SemaphoreType.DMA((n_arrays,))],
        compiler_params=params(megabytes),
        cost_estimate=estimate,
    )(*scalars, *arrays)


def lane_ids(width):
    return lax.broadcasted_iota(jnp.int32, (1, width), 1)


def collect_vectors(where, me, blocks, own, group, vec, table):
    count = len(blocks)
    width = count * own
    table[...] = jnp.zeros_like(table)
    for i, block in enumerate(blocks):
        pair = block[own : own + 2, :].astype(F32)
        table[0, pl.ds(where[i], 1), :] = pair[0:1]
        table[1, pl.ds(where[i], 1), :] = pair[1:2]
    lanes = lax.broadcasted_iota(jnp.int32, (count, width), 1)
    rows = lax.broadcasted_iota(jnp.int32, (count, width), 0)
    mine = (lanes >= rows * own) & (lanes < (rows + 1) * own)
    base = table[0]
    shifted_base = [base] + [pltpu.roll(base, k * own, 1) for k in range(1, count)]

    def whole(index, shifted=None):
        shifted = shifted or shifted_base
        picked = jnp.zeros((count, width), F32)
        for k in range(count):
            here = mine & (rows == (k + index) % count)
            picked = jnp.where(here, shifted[k], picked)
        return jnp.sum(picked, 0, keepdims=True)

    gain1, bias1, qb, vb, bo, gain2, bias2, bd = (whole(i) for i in range(8))
    lane = lane_ids(width)
    qb = pltpu.roll(qb, lax.rem(width - me * group, width), 1)
    vb = pltpu.roll(vb, lax.rem(width + 2 * group - me * group, width), 1)
    bias = jnp.where(lane < group, qb, 0.0)
    bias = jnp.where((lane >= 2 * group) & (lane < 3 * group), vb, bias)
    units = pltpu.roll(table[1], lax.rem(width - me * own, width), 1)
    shifted = [units] + [pltpu.roll(units, k * own, 1) for k in range(1, count)]
    bu = whole(0, shifted)
    for i, row in enumerate((gain1, bias1, bias, bo, gain2, bias2, bd, bu)):
        vec[i : i + 1, :] = row


def units_kernel(own, place_ref, up, down, pair):
    me = place_ref[0]
    count = up.shape[1] // (4 * own)
    for s in range(4):

        @pl.when(me == s)
        def _(s=s):
            for f in range(count):
                start = (4 * f + s) * own
                pair[:own, f * own : (f + 1) * own] = up[:, start : start + own]
            pair[own:, :] = down[s * own : (s + 1) * own, :]


def own_units(me, up, down):
    own, width = up.shape[0], down.shape[1]
    return run(
        functools.partial(units_kernel, own),
        [me],
        [up, down],
        (jax.ShapeDtypeStruct((2 * own, width), BF),),
        [],
        8,
        3.0,
    )[0]


def project_kernel(ring, own, group, rows, *refs):
    where, place_ref = refs[0], refs[1]
    x_refs = refs[2:6]
    n_blocks = 8 if ring else 1
    blocks = refs[6 : 6 + n_blocks]
    rest = refs[6 + n_blocks :]
    if not ring:
        vec_in, rest = rest[0], rest[1:]
    act, queries, keys, values, k_turned, v_turned, w, w_col, vec, kept, table = rest
    me = place_ref[0]
    heads = group // HD
    if ring:
        collect_vectors(where, me, blocks, own, group, vec, table)
    else:
        vec[...] = vec_in[...]
    if ring:
        for i, block in enumerate(blocks):
            start = pl.multiple_of(where[i] * own, own)
            w[pl.ds(start, own), :] = block[:own, : 3 * group]
            w_col[pl.ds(start, own), :] = block[:own, 3 * group :]
    else:
        w[...] = blocks[0][...]
        w_col[...] = jnp.zeros_like(w_col)
    gain, shift, bias = vec[0:1, :], vec[1:2, :], vec[2:3, : 3 * group]
    for k in range(4):
        here = slice(k * rows, (k + 1) * rows)
        values_in = x_refs[k][...]
        kept[here, :] = values_in
        xhat, _ = normalise(values_in.astype(F32))
        block = (xhat * gain + shift).astype(BF)
        act[here, :] = block
        qkv = (dot(block, w[...]) + bias).astype(BF)
        queries[here, :] = qkv[:, :group] * jnp.asarray(HD ** (-0.5), BF)
        for head in range(heads):
            keys[head, here, :] = qkv[:, group + head * HD : group + (head + 1) * HD]
            values[head, here, :] = qkv[:, 2 * group + head * HD : 2 * group + (head + 1) * HD]
        k_turned[:, here] = qkv[:, group : 2 * group].T
        v_turned[:, here] = qkv[:, 2 * group : 3 * group].T


def project(where, me, pieces, blocks, vec, own, group):
    rows, width = pieces[0].shape
    frames = 4 * rows
    heads = group // HD
    ring = len(blocks) > 1
    out_shape = (
        jax.ShapeDtypeStruct((frames, width), BF),
        jax.ShapeDtypeStruct((frames, group), BF),
        jax.ShapeDtypeStruct((heads, frames, HD), BF),
        jax.ShapeDtypeStruct((heads, frames, HD), BF),
        jax.ShapeDtypeStruct((group, frames), BF),
        jax.ShapeDtypeStruct((group, frames), BF),
        jax.ShapeDtypeStruct((width, 3 * group), BF),
        jax.ShapeDtypeStruct((width, group), BF),
        jax.ShapeDtypeStruct((8, width), F32),
        jax.ShapeDtypeStruct((frames, width), BF),
    )
    args = [where, me, *pieces, *blocks] + ([] if ring else [vec])
    return run(
        functools.partial(project_kernel, ring, own, group, rows),
        args[:2],
        args[2:],
        out_shape,
        [pltpu.VMEM((2, 8, width), F32)],
        16,
        9.0,
        direct=True,
    )


def attend_kernel(group, rows, part, queries, keys, v_turned, first, second, lse):
    heads = group // HD
    lse[...] = jnp.zeros_like(lse)
    for t, out in enumerate((first, second)):
        turned = []
        for head in range(heads):
            start = (2 * part + t) * rows
            query = queries[start : start + rows, head * HD : (head + 1) * HD]
            scores = dot_nt(keys[head], query)
            top = jnp.max(scores, 0, keepdims=True)
            e = jnp.exp(scores - top)
            total = jnp.sum(e, 0, keepdims=True)
            lse[head : head + 1, t * rows : (t + 1) * rows] = top + jnp.log(total)
            p = (e * (1.0 / total)).astype(BF)
            turned.append(dot(v_turned[head * HD : (head + 1) * HD, :], p))
        out[...] = jnp.concatenate(turned, 0).T.astype(BF)


def attend(part, queries, keys, v_turned):
    frames, group = queries.shape
    rows = frames // 4
    return run(
        functools.partial(attend_kernel, group, rows, part),
        [],
        [queries, keys, v_turned],
        (
            jax.ShapeDtypeStruct((rows, group), BF),
            jax.ShapeDtypeStruct((rows, group), BF),
            jax.ShapeDtypeStruct((8, 2 * rows), F32),
        ),
        [],
        10,
        7.5,
    )


def mix_kernel(own, group, rows, *refs):
    where, place_ref, vec, x = refs[:4]
    o_refs = refs[4:8]
    blocks, (h, act, w) = refs[8:-3], refs[-3:]
    me = place_ref[0]
    if len(blocks) == 1:
        w[...] = blocks[0][...]
    else:
        for k, block in enumerate(blocks):
            for c in range(4):

                @pl.when((me ^ k) == c)
                def _(block=block, c=c):
                    w[:, c * group : (c + 1) * group] = block[...]

    total = x[...].astype(F32) + vec[3:4, :]
    for k in range(4):
        start = pl.multiple_of((me ^ k) * group, group)
        total = total + dot(o_refs[k][:rows, :], w[pl.ds(start, group), :])
    h[...] = total
    xhat, _ = normalise(total)
    act[...] = (xhat * vec[4:5, :] + vec[5:6, :]).astype(BF)


def mix(where, me, vec, x, pieces, blocks, own, group):
    rows, width = x.shape
    args = [where, me, vec, x, *pieces, *blocks]
    return run(
        functools.partial(mix_kernel, own, group, rows),
        args[:2],
        args[2:],
        (
            jax.ShapeDtypeStruct((rows, width), F32),
            jax.ShapeDtypeStruct((rows, width), BF),
            jax.ShapeDtypeStruct((width, width), BF),
        ),
        [],
        10,
        6.0,
    )


def feed_kernel(n_up, n_down, own, rows, *refs):
    where, vec, a0, a1, dy0, dy1 = refs[:6]
    ups = refs[6 : 6 + n_up]
    downs = refs[6 + n_up : 6 + n_up + n_down]
    g, du, first, second, total, w_up, w_down = refs[6 + n_up + n_down :]
    if n_down:
        w_up[...] = ups[0][...]
        w_down[...] = downs[0][...]
    elif len(ups) == 1:
        for i in range(w_up.shape[0] // own):
            here = slice(i * own, (i + 1) * own)
            w_up[here, :] = ups[0][2 * i * own : (2 * i + 1) * own, :]
            w_down[here, :] = ups[0][(2 * i + 1) * own : (2 * i + 2) * own, :]
    else:
        for i, block in enumerate(ups):
            start = pl.multiple_of(where[i] * own, own)
            skip = block.shape[0] - 2 * own
            w_up[pl.ds(start, own), :] = block[skip : skip + own, :]
            w_down[pl.ds(start, own), :] = block[skip + own :, :]
    bias = vec[7:8, :]
    total[...] = jnp.zeros_like(total)
    chunk = rows // 2
    for part, (a, dy, out) in enumerate(((a0, dy0, first), (a1, dy1, second))):
        for c in range(2):
            here = slice(c * chunk, (c + 1) * chunk)
            there = slice(part * rows + c * chunk, part * rows + (c + 1) * chunk)
            u = dot(a[here, :], w_up[...]) + bias
            cdf = 0.5 * (1.0 + lax.erf(u * (0.5**0.5)))
            pdf = jnp.exp(-0.5 * u * u) * ((2.0 * jnp.pi) ** (-0.5))
            g[there, :] = (u * cdf).astype(BF)
            grad = (dot_nt(dy[here, :], w_down[...]) * (cdf + u * pdf)).astype(BF)
            du[there, :] = grad
            total[0:1, :] += jnp.sum(grad.astype(F32), 0, keepdims=True)
            out[here, :] = dot_nt(grad, w_up[...]).astype(out.dtype)


def feed(where, vec, acts, dys, ups, downs, own):
    rows, width = acts[0].shape
    hidden = ups[0].shape[1]
    assert width == hidden
    args = [where, vec, *acts, *dys, *ups, *downs]
    return run(
        functools.partial(feed_kernel, len(ups), len(downs), own, rows),
        args[:1],
        args[1:],
        (
            jax.ShapeDtypeStruct((2 * rows, hidden), BF),
            jax.ShapeDtypeStruct((2 * rows, hidden), BF),
            jax.ShapeDtypeStruct((rows, width), F32),
            jax.ShapeDtypeStruct((rows, width), BF),
            jax.ShapeDtypeStruct((8, hidden), F32),
            jax.ShapeDtypeStruct((width, hidden), BF),
            jax.ShapeDtypeStruct((hidden, width), BF),
        ),
        [],
        18,
        8.2,
    )


def feed_out_kernel(rows, g_a, g_b, w, first, third, sent):
    for k in (1, 3, 0, 2):
        here = slice((k % 2) * rows, (k % 2 + 1) * rows)
        part = dot((g_a if k < 2 else g_b)[here, :], w[...])
        if k == 0:
            first[...] = part
        elif k == 2:
            third[...] = part
        else:
            sent[(k // 2) * rows : (k // 2 + 1) * rows, :] = part.astype(BF)


def feed_out(gs, w):
    rows = gs[0].shape[0] // 2
    width = w.shape[1]
    return run(
        functools.partial(feed_out_kernel, rows),
        [],
        [*gs, w],
        (
            jax.ShapeDtypeStruct((rows, width), F32),
            jax.ShapeDtypeStruct((rows, width), F32),
            jax.ShapeDtypeStruct((2 * rows, width), BF),
        ),
        [],
        10,
        3.0,
    )


def turn_kernel(*refs):
    vec, h, dy, part, near, far = refs[1:7]
    dh, db, sums = refs[7:]
    da = part[...] + near[...].astype(F32) + far[...].astype(F32)
    xhat, rstd = normalise(h[...])
    cot = dy[...].astype(F32)
    grad = cot + norm_back(da, vec[4:5, :], xhat, rstd)
    dh[...] = grad
    low = grad.astype(BF)
    db[...] = low
    sums[...] = jnp.zeros_like(sums)
    sums[0:1, :] = jnp.sum(low.astype(F32), 0, keepdims=True)
    sums[1:2, :] = jnp.sum(da * xhat, 0, keepdims=True)
    sums[2:3, :] = jnp.sum(da, 0, keepdims=True)
    sums[3:4, :] = jnp.sum(cot, 0, keepdims=True)


def turn(me, vec, h, dy, part, near, far):
    rows, width = h.shape
    return run(
        turn_kernel,
        [me],
        [vec, h, dy, part, near, far],
        (
            jax.ShapeDtypeStruct((rows, width), F32),
            jax.ShapeDtypeStruct((rows, width), BF),
            jax.ShapeDtypeStruct((8, width), F32),
        ),
        [],
        10,
        3.0,
    )


def back_tiles(me, group, rows, part, qkv, lse, db_refs, w, dk, dv, dq, skip):
    queries, keys, values, k_turned = qkv
    heads = group // HD
    for t in range(2):
        start = (2 * part + t) * rows
        turned = []
        w_own = w[pl.ds(pl.multiple_of(me * group, group), group), :]
        d_all = dot_nt(db_refs[t][...], w_own).astype(BF)
        for head in range(heads):
            here = slice(head * HD, (head + 1) * HD)
            query = queries[start : start + rows, here]
            d_out = d_all[:, here]
            scores = dot_nt(keys[head], query)
            p = jnp.exp(scores - lse[head : head + 1, t * rows : (t + 1) * rows])
            dv[head] += dot(p.astype(BF), d_out)
            dp = dot_nt(values[head], d_out)
            inner = jnp.sum(p * dp, 0, keepdims=True)
            ds = (p * (dp - inner)).astype(BF)
            dk[head] += dot(ds, query)
            turned.append(dot(k_turned[here, :], ds))
        dq[skip + t * rows : skip + (t + 1) * rows, :group] = (
            jnp.concatenate(turned, 0).T * HD ** (-0.5)
        ).astype(BF)


def back_first_kernel(group, rows, place_ref, *refs):
    qkv, (lse, db0, db1, w, dq, dk, dv) = refs[:4], refs[4:]
    dk[...] = jnp.zeros_like(dk)
    dv[...] = jnp.zeros_like(dv)
    back_tiles(place_ref[0], group, rows, 0, qkv, lse, (db0, db1), w, dk, dv, dq, 0)


def back_first(me, queries, keys, values, k_turned, lse, dbs, w):
    frames, group = queries.shape
    heads = group // HD
    total = jax.ShapeDtypeStruct((heads, frames, HD), F32)
    return run(
        functools.partial(back_first_kernel, group, frames // 4),
        [me],
        [queries, keys, values, k_turned, lse, *dbs, w],
        (jax.ShapeDtypeStruct((frames // 2, group), BF), total, total),
        [],
        18,
        12.0,
    )


def back_second_kernel(group, rows, place_ref, *refs):
    qkv, (lse, w, dq_first, dk_first, dv_first, db2, db3) = refs[:4], refs[4:11]
    dqkv, dk, dv = refs[11:]
    heads = group // HD
    dk[...] = dk_first[...]
    dv[...] = dv_first[...]
    dqkv[: 2 * rows, :group] = dq_first[...]
    dbs = (db2, db3)
    back_tiles(place_ref[0], group, rows, 1, qkv, lse, dbs, w, dk, dv, dqkv, 2 * rows)
    dqkv[:, group : 2 * group] = jnp.concatenate([dk[i] for i in range(heads)], 1).astype(BF)
    dqkv[:, 2 * group :] = jnp.concatenate([dv[i] for i in range(heads)], 1).astype(BF)


def back_second(me, queries, keys, values, k_turned, lse, w, first, dbs):
    frames, group = queries.shape
    heads = group // HD
    return run(
        functools.partial(back_second_kernel, group, frames // 4),
        [me],
        [queries, keys, values, k_turned, lse, w, *first, *dbs],
        (jax.ShapeDtypeStruct((frames, 3 * group), BF),),
        [pltpu.VMEM((heads, frames, HD), F32), pltpu.VMEM((heads, frames, HD), F32)],
        20,
        12.0,
    )[0]


def feed_grads_kernel(own, rows, *refs):
    acts, dys = refs[:4], refs[4:8]
    g_a, g_b, du_a, du_b = refs[8:12]
    out = refs[12]
    up, down = 0.0, 0.0
    for k in range(4):
        here = slice((k % 2) * rows, (k % 2 + 1) * rows)
        up = up + dot_tn(acts[k][...], (du_a if k < 2 else du_b)[here, :])
    for f in range(out.shape[0]):
        out[f, :own, :] = up[f * own : (f + 1) * own, :].astype(BF)
    for k in range(4):
        here = slice((k % 2) * rows, (k % 2 + 1) * rows)
        down = down + dot_tn((g_a if k < 2 else g_b)[here, :], dys[k][...])
    for f in range(out.shape[0]):
        out[f, own:, :] = down[f * own : (f + 1) * own, :].astype(BF)


def feed_grads(acts, dys, gs, dus, own):
    rows, width = acts[0].shape
    return run(
        functools.partial(feed_grads_kernel, own, rows),
        [],
        [*acts, *dys, *gs, *dus],
        (jax.ShapeDtypeStruct((width // own, 2 * own, width), BF),),
        [],
        20,
        9.0,
    )[0]


def out_grads_kernel(own, group, *refs):
    o_refs, db_refs, blocks = refs[1:5], refs[5:9], refs[9]
    total = 0.0
    for k in range(4):
        total = total + dot_tn(o_refs[k][...], db_refs[k][...])
    for j in range(group // own):
        for t in range(4):
            blocks[j * 4 + t] = total[j * own : (j + 1) * own, t * group : (t + 1) * group]


def out_grads(me, os, dbs, own):
    group = os[0].shape[1]
    return run(
        functools.partial(out_grads_kernel, own, group),
        [me],
        [*os, *dbs],
        (jax.ShapeDtypeStruct((group // own * 4, own, group), F32),),
        [],
        12,
        3.0,
    )


def plane_kernel(own, place_ref, keep, got, *outs):
    plane = place_ref[2]
    for step, out in enumerate(outs):
        z = plane ^ step
        total = keep[z, :own, :] + got[z, :own, :].astype(F32)
        lines = keep[z, own:, :] + got[z, own : own + 8, :].astype(F32)
        lines = lines + got[z, own + 8 :, :].astype(F32)
        if step == 0:
            out[:own, :] = total
            out[own:, :] = lines
        else:
            out[:own, :] = total.astype(BF)
            high, low = split_low(lines)
            out[own : own + 8, :] = high
            out[own + 8 :, :] = low


def plane_parts(me, keep, got):
    planes, height, width = keep.shape
    out_shape = [jax.ShapeDtypeStruct((height, width), F32)]
    out_shape += [jax.ShapeDtypeStruct((height + 8, width), BF)] * (planes - 1)
    return run(
        functools.partial(plane_kernel, height - 8),
        [me],
        [keep, got],
        tuple(out_shape),
        [],
        12,
        2.2,
    )


def split_low(value):
    high = value.astype(BF)
    return high, (value - high.astype(F32)).astype(BF)


def close_kernel(own, group, rows, split, place_ref, dqkv, act, w, x, *refs):
    o_refs, db_refs = refs[:4], refs[4:8]
    sums2, usum_a, usum_b = refs[8:11]
    if split:
        keep, give, first, third, sent, table, lines, grads = refs[11:]
    else:
        grads, first, third, sent, sums = refs[11:]
    width = w.shape[0]
    gain_sum, shift_sum = 0.0, 0.0
    for k in (1, 3, 0, 2):
        part = dot_nt(dqkv[k * rows : (k + 1) * rows, :], w[...])
        xhat, _ = normalise(x[k * rows : (k + 1) * rows, :].astype(F32))
        gain_sum = gain_sum + jnp.sum(part * xhat, 0, keepdims=True)
        shift_sum = shift_sum + jnp.sum(part, 0, keepdims=True)
        if k == 0:
            first[...] = part
        elif k == 2:
            third[...] = part
        else:
            sent[(k // 2) * rows : (k // 2 + 1) * rows, :] = part.astype(BF)
    dsum = jnp.sum(dqkv[...].astype(F32), 0, keepdims=True)
    if not split:
        sums[...] = jnp.zeros_like(sums)
        sums[0:1, :] = gain_sum
        sums[1:2, :] = shift_sum
        sums[2:3, : 3 * group] = dsum
        grads[...] = dot_tn(act[...], dqkv[...])
        return
    me, side = place_ref[0], place_ref[1]
    out = 0.0
    for k in range(4):
        out = out + dot_tn(o_refs[k][...], db_refs[k][...])
    for j in range(2):
        for t in range(4):
            start = (j * 4 + t) * own
            grads[start : start + own, 3 * group :] = out[
                j * own : (j + 1) * own, t * group : (t + 1) * group
            ]
    grads[:, : 3 * group] = dot_tn(act[...], dqkv[...])
    count = width // own
    lane = lane_ids(width)
    table[0:1, :] = gain_sum
    table[1:2, :] = shift_sum
    table[3:4, :] = jnp.zeros((1, width), F32)
    table[3:4, : 3 * group] = dsum
    spread = table[3:4, :]
    query = jnp.where(lane < group, spread, 0.0)
    value = jnp.where(lane < group, pltpu.roll(spread, 2 * group, 1), 0.0)
    table[2:3, :] = pltpu.roll(query, me * group, 1)
    table[3:4, :] = pltpu.roll(value, me * group, 1)
    table[4:8, :] = sums2[0:4, :]
    base = table[...]
    shifted = [base] + [pltpu.roll(base, k * own, 1) for k in range(1, count)]
    lanes = lax.broadcasted_iota(jnp.int32, (count, width), 1)
    ids = lax.broadcasted_iota(jnp.int32, (count, width), 0)
    mine = (lanes >= ids * own) & (lanes < (ids + 1) * own)
    units = pltpu.roll(usum_a[0:1, :] + usum_b[0:1, :], me * own, 1)
    inside = (lane >= me * own) & (lane < (me + 1) * own)
    for f in range(count):
        picked = jnp.zeros((count, width), F32)
        for k in range(count):
            picked = jnp.where(mine & (ids == (f + k) % count), shifted[k], picked)
        lines[f, 0:1, :] = jnp.sum(picked, 0, keepdims=True)
        turned = units if f == 0 else pltpu.roll(units, width - f * own, 1)
        lines[f, 1:2, :] = jnp.where(inside, turned, 0.0)
    for z in range(count // 2):
        mine_f, other = 2 * z + side, 2 * z + 1 - side
        keep[z, :own, :] = grads[pl.ds(pl.multiple_of(mine_f * own, own), own), :]
        keep[z, own:, :] = lines[mine_f]
        rest = grads[pl.ds(pl.multiple_of(other * own, own), own), :]
        give[z, :own, :] = rest.astype(BF)
        high, low = split_low(lines[other])
        give[z, own : own + 8, :] = high
        give[z, own + 8 :, :] = low


def close(me, dqkv, act, w, x, os, dbs, sums2, usum_a, usum_b, own, planes):
    rows, width = x.shape[0] // 4, x.shape[1]
    group = width // 4
    split = planes > 1
    out_shape = (
        jax.ShapeDtypeStruct((rows, width), F32),
        jax.ShapeDtypeStruct((rows, width), F32),
        jax.ShapeDtypeStruct((2 * rows, width), BF),
    )
    if split:
        out_shape = (
            jax.ShapeDtypeStruct((planes, own + 8, width), F32),
            jax.ShapeDtypeStruct((planes, own + 16, width), BF),
        ) + out_shape
        scratch = [
            pltpu.VMEM((8, width), F32),
            pltpu.VMEM((2 * planes, 8, width), F32),
            pltpu.VMEM((width, width), F32),
        ]
    else:
        out_shape = (
            (jax.ShapeDtypeStruct((width, 3 * group), F32),)
            + out_shape
            + (jax.ShapeDtypeStruct((8, width), F32),)
        )
        scratch = []
    return run(
        functools.partial(close_kernel, own, group, rows, split),
        [me],
        [dqkv, act, w, x, *os, *dbs, sums2, usum_a, usum_b],
        out_shape,
        scratch,
        30,
        10.5,
    )


def finish_kernel(vec, x, dh, part, near, far, out):
    da = part[...] + near[: part.shape[0], :].astype(F32) + far[...].astype(F32)
    xhat, rstd = normalise(x[...].astype(F32))
    out[...] = (dh[...] + norm_back(da, vec[0:1, :], xhat, rstd)).astype(BF)


def finish(vec, x, dh, part, near, far):
    return run(
        finish_kernel,
        [],
        [vec, x, dh, part, near, far],
        (jax.ShapeDtypeStruct(x.shape, BF),),
        [],
        8,
        3.0,
    )[0]


def share_kernel(own, group, place_ref, own_sum, got1, got2, got3, feed, *outs):
    me = place_ref[0]
    total = own_sum[:own, :]
    lines = own_sum[own:, :]
    for got in (got1, got2, got3):
        total = total + got[:own, :].astype(F32)
        lines = lines + got[own : own + 8, :].astype(F32) + got[own + 8 :, :].astype(F32)
    low = total.astype(BF)
    rows = [lines[0:1, i * group : (i + 1) * group] for i in range(4)]
    rows += [lines[1:2, i * group : (i + 1) * group] for i in range(2)]
    rows += [jnp.zeros((2, group), F32)]
    high, rest = split_low(jnp.concatenate(rows, 0))
    orders = ((0, 1, 2), (1, 0, 2), (1, 2, 0), (2, 1, 0))
    for k in range(4):
        outs[k][:8, :] = high
        outs[k][8:16, :] = rest
    for s in range(4):

        @pl.when(me == s)
        def _(s=s):
            for k in range(4):
                unit = orders[s][min(k, 2)]
                c = s ^ k
                outs[k][16 : 16 + own, :] = low[:, unit * group : (unit + 1) * group]
                outs[k][16 + own :, :] = feed[:, c * group : (c + 1) * group]

    outs[4][...] = low[:, 3 * group :]


def share(me, own_sum, arrived, feed):
    own, width = feed.shape[0] // 2, feed.shape[1]
    group = width // 4
    piece = jax.ShapeDtypeStruct((16 + 3 * own, group), BF)
    return run(
        functools.partial(share_kernel, own, group),
        [me],
        [own_sum, *arrived, feed],
        (piece,) * 4 + (jax.ShapeDtypeStruct((own, group), BF),),
        [],
        10,
        3.0,
    )


def settle_kernel(own, group, place_ref, *refs):
    pieces, out = refs[:4], refs[4]
    qkv_grad, up_grad, down_grad, out_grad, sums = refs[5:]
    me = place_ref[0]
    half = group // 2
    total = 0.0
    for piece in pieces:
        total = total + piece[:8, :].astype(F32) + piece[8:16, :].astype(F32)
    sums[...] = total
    out_grad[...] = out[...].astype(F32)
    for s in range(4):

        @pl.when(me == s)
        def _(s=s):
            for k in range(4):
                c = s ^ k
                if k < 3:
                    spot = k if s % 2 == 0 else 2 - k
                    qkv_grad[:, spot * group : (spot + 1) * group] = pieces[k][
                        16 : 16 + own, :
                    ].astype(F32)
                up = pieces[k][16 + own : 16 + 2 * own, :].astype(F32)
                for j in range(2):
                    start = (4 * j + c) * half
                    up_grad[:, start : start + half] = up[:, j * half : (j + 1) * half]
                down_grad[c * own : (c + 1) * own, :] = pieces[k][16 + 2 * own :, :].astype(F32)


def settle(me, pieces, out):
    own, group = out.shape
    return run(
        functools.partial(settle_kernel, own, group),
        [me],
        [*pieces, out],
        (
            jax.ShapeDtypeStruct((own, 3 * group), F32),
            jax.ShapeDtypeStruct((own, 4 * group), F32),
            jax.ShapeDtypeStruct((4 * own, group), F32),
            jax.ShapeDtypeStruct((own, group), F32),
            jax.ShapeDtypeStruct((8, group), F32),
        ),
        [],
        8,
        3.8,
    )


def body(
    frames_in,
    norm1_gain,
    norm1_bias,
    qkv_weight,
    query_bias,
    value_bias,
    out_weight,
    out_bias,
    norm2_gain,
    norm2_bias,
    up_weight,
    up_bias,
    down_weight,
    down_bias,
    cotangent,
):
    count = lax.axis_size("fsdp")
    q = count // GROUPS
    s = lax.axis_index("seq")
    f = lax.axis_index("fsdp")
    width = frames_in.shape[2]
    rows = frames_in.shape[0] * frames_in.shape[1]
    group = width // GROUPS
    own = qkv_weight.shape[0]
    hidden_all = up_weight.shape[1]
    hidden = hidden_all // GROUPS
    hid_own = down_weight.shape[0]
    ring = count == 8
    planes = count // 2 if ring else 1
    me = jnp.stack([s, f % 2, f // 2, f % GROUPS]).astype(jnp.int32)

    x = frames_in.reshape(rows, width)
    dy = cotangent.reshape(rows, width)

    vectors = jnp.concatenate(
        [
            norm1_gain,
            norm1_bias,
            query_bias,
            value_bias,
            out_bias,
            norm2_gain,
            norm2_bias,
            down_bias,
            up_bias,
        ]
    )
    lines = -(-vectors.shape[0] // width)
    padded = jnp.pad(vectors, (0, lines * width - vectors.shape[0])).reshape(lines, width)
    qkv_own = lax.dynamic_index_in_dim(
        qkv_weight.reshape(own, 3, GROUPS, group), s, 2, keepdims=False
    ).reshape(own, 3 * group)
    out_own = lax.dynamic_index_in_dim(
        out_weight.reshape(own, GROUPS, group), s, 1, keepdims=False
    )
    packed = jnp.concatenate([jnp.concatenate([qkv_own, out_own], 1), padded], 0)
    if ring:
        vec = None
        x_pieces = [x] + [seq_swap(x, k) for k in (1, 2, 3)]
        where, qkv_blocks = ring_gather(packed, count)
        pair = own_units(me, after(up_weight, *qkv_blocks[1:3]), down_weight)
        up_blocks = [lax.all_gather(pair, "fsdp", axis=0, tiled=True)]
        down_blocks = []
    else:
        where = jnp.zeros((8,), jnp.int32)
        x_pieces = seq_pieces(x)
        up_own = lax.dynamic_index_in_dim(
            up_weight.reshape(own, count, GROUPS, own), s, 2, keepdims=False
        ).reshape(own, hidden)
        down_own = lax.dynamic_slice_in_dim(down_weight, s * own, own, 0)
        first = lax.all_gather(packed, "fsdp", axis=0, tiled=False)
        qkv_blocks = [first[:, :own, : 3 * group].reshape(width, 3 * group)]
        spread = first[:, own:].reshape(count, lines * width).astype(F32)
        gain1, bias1, qb, vb, bo, gain2, bias2, bd = (
            spread[:, i * own : (i + 1) * own].reshape(width) for i in range(8)
        )
        bu = spread[:, 8 * own : 8 * own + hid_own].reshape(hidden_all)
        bias = jnp.concatenate(
            [
                lax.dynamic_slice_in_dim(qb, s * group, group),
                jnp.zeros((group,), F32),
                lax.dynamic_slice_in_dim(vb, s * group, group),
                jnp.zeros((group,), F32),
            ]
        )
        bu = lax.dynamic_index_in_dim(
            bu.reshape(count, GROUPS, own), s, 1, keepdims=False
        ).reshape(hidden)
        vec = jnp.stack([gain1, bias1, bias, bo, gain2, bias2, bd, bu])
        second = lax.all_gather(
            jnp.concatenate([up_own, out_weight, down_own], 0), "fsdp", axis=0, tiled=False
        )
        up_blocks = [second[:, :own].reshape(width, hidden)]
        out_blocks = [second[:, own : 2 * own].reshape(width, width)]
        down_blocks = [second[:, 2 * own :].reshape(hidden, width)]

    act1, queries, keys, values, k_turned, v_turned, w_qkv, w_col, vec, x_kept = project(
        where, me, x_pieces, qkv_blocks, vec, own, group
    )
    if ring:
        out_blocks = [w_col, seq_swap(w_col, 1), seq_swap(w_col, 2)]
    o2, o3, lse_b = attend(1, queries, keys, v_turned)
    far2, far3 = seq_swap(o2, 2), seq_swap(o3, 3)
    queries_a = after(queries, o2)
    if ring:
        out_blocks.append(seq_swap(after(out_blocks[2], o2), 1))
    o0, o1, lse_a = attend(0, queries_a, keys, v_turned)
    o_pieces = [o0, seq_swap(o1, 1), far2, far3]
    pieces = seq_pieces(after(dy, o0))
    h, act2, w_out = mix(where, me, vec, x, o_pieces, out_blocks, own, group)
    a_pieces = [act2, seq_swap(act2, 1), seq_swap(act2, 2)]
    g_a, du_a, part0, part1, usum_a, w_up, w_down = feed(
        where, vec, a_pieces[:2], pieces[:2], up_blocks, down_blocks, own
    )
    a_pieces.append(seq_swap(after(a_pieces[2], g_a), 1))
    near0 = seq_swap(part1, 1)
    g_b, du_b, part2, part3, usum_b, _, _ = feed(
        where, vec, a_pieces[2:], pieces[2:], [w_up], [w_down], own
    )
    near2 = seq_swap(part3, 1)
    far_sum = (part2 + near2.astype(F32)).astype(BF)
    far = seq_swap(far_sum, 2)

    du_late = after(du_b, far_sum)
    feed_parts = feed_grads(a_pieces, pieces, (g_a, g_b), (du_a, du_late), own)
    feed_total = fsdp_reduce(feed_parts)
    far = after(far, feed_parts)
    dh, db, sums2 = turn(me, vec, h, dy, part0, near0, far)
    db_pieces = [db, seq_swap(db, 1), seq_swap(db, 2)]
    y_parts = feed_out((g_a, after(g_b, db)), w_down)
    lse_a = after(lse_a, y_parts[0])
    back_a = back_first(me, queries, keys, values, k_turned, lse_a, db_pieces[:2], w_out)
    db_pieces.append(seq_swap(after(db_pieces[2], back_a[0]), 1))
    y_near = seq_swap(after(y_parts[2], back_a[0]), 1)
    y_sum = (y_parts[1] + y_near[rows:].astype(F32)).astype(BF)
    lse_b = after(lse_b, back_a[0])
    dqkv = back_second(
        me, queries, keys, values, k_turned, lse_b, w_out, back_a, db_pieces[2:]
    )
    y_far = seq_swap(after(y_sum, back_a[0]), 2)
    os = (o0, o1, o2, o3)
    closed = close(
        me, dqkv, act1, w_qkv, x_kept, os, db_pieces, sums2, usum_a, usum_b, own, planes
    )
    if ring:
        keep, give, part0, part2, sent = closed
        got = side_swap(give, count)
    else:
        grad_heads, part0, part2, sent, sums1 = closed
    near = seq_swap(sent, 1)
    far_sum = (part2 + near[rows:].astype(F32)).astype(BF)
    if ring:
        got = after(got, far_sum)
        own_sum, *sends = plane_parts(me, keep, got)
        arrived = plane_swaps(sends, count)
    far1 = seq_swap(far_sum, 2)
    layer_out = h + (y_parts[0] + y_near[:rows].astype(F32) + y_far.astype(F32)) + vec[6]
    layer_out = layer_out.astype(BF).reshape(frames_in.shape)
    input_grad = finish(vec, x, dh, part0, near, far1).reshape(frames_in.shape)
    if ring:
        *shares, out_block = share(me, own_sum, arrived, feed_total)
        shares = [shares[0]] + [seq_swap(shares[step], step) for step in (1, 2, 3)]
        out_block = to_owners(out_block, count, 0)
        grad_qkv, grad_up, grad_down, grad_out, vectors = settle(me, shares, out_block)
        vectors = vectors.reshape(16, own)
        g_gain1, g_bias1, g_query, g_value, g_outb, g_gain2, g_bias2, g_downb = (
            vectors[i] for i in range(8)
        )
        g_upb = vectors[8:12].reshape(hid_own)
    else:
        units = fsdp_reduce(grad_heads.reshape(count, own, 3 * group)).astype(BF)
        units = units.reshape(own, 3, group)
        order = jnp.array([[0, 1, 2], [1, 0, 2], [1, 2, 0], [2, 1, 0]], jnp.int32)[s]
        got = [lax.dynamic_index_in_dim(units, order[k], 1, keepdims=False) for k in range(3)]
        got = [got[0], seq_swap(got[1], 1), seq_swap(got[2], 2)]
        odd = s % 2 == 1
        grad_qkv = jnp.concatenate(
            [jnp.where(odd, got[2], got[0]), got[1], jnp.where(odd, got[0], got[2])], 1
        ).astype(F32)
        grad_up, grad_down = feed_total[:own].astype(F32), feed_total[own:]
        out_parts = out_grads(me, [o0, o1, o2, o3], db_pieces, own)
        grad_out = to_owners(fsdp_reduce(out_parts[0]).astype(BF), count, 0).astype(F32)
        grad_down = lax.all_to_all(
            grad_down, "seq", split_axis=1, concat_axis=0, tiled=True
        ).astype(F32)
        grad_up = lax.all_to_all(
            grad_up.astype(BF).reshape(own, GROUPS, q, own), "seq", split_axis=1, concat_axis=1
        )
        grad_up = grad_up.transpose(0, 2, 1, 3).reshape(own, hidden).astype(F32)

        def placed(values, size):
            return lax.dynamic_update_slice_in_dim(
                jnp.zeros((size,), F32), values, s * values.shape[0], 0
            ).reshape(count, size // count)

        sums = [
            sums1[0].reshape(count, own),
            sums1[1].reshape(count, own),
            placed(sums1[2, :group], width),
            placed(sums1[2, 2 * group : 3 * group], width),
            sums2[0].reshape(count, own),
            sums2[1].reshape(count, own),
            sums2[2].reshape(count, own),
            sums2[3].reshape(count, own),
            lax.dynamic_update_slice_in_dim(
                jnp.zeros((count, hid_own), F32),
                (usum_a[0] + usum_b[0]).reshape(count, own),
                s * own,
                1,
            ),
        ]
        total = lax.psum(fsdp_reduce(jnp.concatenate(sums, 1)), "seq")
        g_gain1, g_bias1, g_query, g_value, g_outb, g_gain2, g_bias2, g_downb = (
            total[i * own : (i + 1) * own] for i in range(8)
        )
        g_upb = total[8 * own :]

    return (
        layer_out,
        input_grad,
        g_gain1,
        g_bias1,
        grad_qkv,
        g_query,
        g_value,
        grad_out,
        g_outb,
        g_gain2,
        g_bias2,
        grad_up,
        g_upb,
        grad_down,
        g_downb,
    )


def solution(mesh):
    tokens = P("fsdp", "seq", None)
    vector = P("fsdp")
    matrix = P("fsdp", None)
    summed = P("fsdp", "seq")
    return jax.shard_map(
        body,
        mesh=mesh,
        in_specs=(
            tokens,
            vector,
            vector,
            matrix,
            vector,
            vector,
            matrix,
            vector,
            vector,
            vector,
            matrix,
            vector,
            matrix,
            vector,
            tokens,
        ),
        out_specs=(
            tokens,
            tokens,
            vector,
            vector,
            summed,
            vector,
            vector,
            summed,
            vector,
            vector,
            vector,
            summed,
            vector,
            summed,
            vector,
        ),
        check_vma=False,
    )
```

profile of v0, /device:TPU:0, one launch (start us, length us, event | category | flops | bytes accessed | tf_op | source)
XLA Modules:
  0.0 226.2 jit_solution(9794729706826703139)
XLA Ops:
  10.4 3.0 %collective-permute-start.4 = (bf16[98,768]{1,0:T(8,128)(2,1)S(1)}, bf16[98,768]{1,0:T(8,128)(2,1)S(1)}, u32[]{:S(2)}, u32[]{:S(2)}) collective-permute-start(bf16[98,768]{1,0:T(8,128)(2,1)S(1)} %pad_maximum_fusion.refs_6_), channel_id=1, source_target_pairs={{8,0},{16,8},{24,16},{28,24},{20,28},{12,20},{4,12},{0,4},{9,1},{1... | collective-permute-start | bytes 451592 | tf_op jit(solution)/shard_map/ppermute | solution.py:73
  13.6 4.0 %collective-permute-done.4.refs_8_ = bf16[98,768]{1,0:T(8,128)(2,1)S(1)} collective-permute-done((bf16[98,768]{1,0:T(8,128)(2,1)S(1)}, bf16[98,768]{1,0:T(8,128)(2,1)S(1)}, u32[]{:S(2)}, u32[]{:S(2)}) %collective-permute-start.4) | collective-permute-done | bytes 150560 | tf_op jit(solution)/shard_map/ppermute | solution.py:73
  28.7 4.1 %collective-permute-done.8.refs_12_ = bf16[98,768]{1,0:T(8,128)(2,1)S(1)} collective-permute-done((bf16[98,768]{1,0:T(8,128)(2,1)S(1)}, bf16[98,768]{1,0:T(8,128)(2,1)S(1)}, u32[]{:S(2)}, u32[]{:S(2)}) %collective-permute-start.8) | collective-permute-done | bytes 150560 | tf_op jit(solution)/shard_map/ppermute | solution.py:73
  32.9 2.5 %collective-permute-start.10 = (bf16[50,768]{1,0:T(8,128)(2,1)S(1)}, bf16[50,768]{1,0:T(8,128)(2,1)S(1)}, u32[]{:S(2)}, u32[]{:S(2)}) collective-permute-start(bf16[50,768]{1,0:T(8,128)(2,1)S(1)} %slice.64), channel_id=1, source_target_pairs={{8,0},{16,8},{24,16},{28,24},{20,28},{12,20},{4,12},{0,4},{9,1},{1... | collective-permute-start | bytes 230408 | tf_op jit(solution)/shard_map/ppermute | solution.py:76
  36.6 4.2 %collective-permute-done.9 = bf16[48,768]{1,0:T(8,128)(2,1)S(1)} collective-permute-done((bf16[48,768]{1,0:T(8,128)(2,1)S(1)}, bf16[48,768]{1,0:T(8,128)(2,1)S(1)}, u32[]{:S(2)}, u32[]{:S(2)}) %collective-permute-start.9) | collective-permute-done | bytes 73760 | tf_op jit(solution)/shard_map/ppermute | solution.py:76
  42.3 3.4 %shard_map.289 = (bf16[1024,768]{1,0:T(8,128)(2,1)S(1)}, bf16[1024,192]{1,0:T(8,128)(2,1)S(1)}, bf16[3,1024,64]{2,1,0:T(8,128)(2,1)S(1)}, bf16[3,1024,64]{2,1,0:...) custom-call(s32[8]{0:T(128)S(1)} %gather_fusion, ...), custom_call_target="tpu_custom_call" | custom-call | flops 8999999488 | bytes 1048576 | tf_op jit(solution)/shard_map/pallas_call | solution.py:139
  47.8 5.3 %shard_map.290 = (bf16[256,192]{1,0:T(8,128)(2,1)S(1)}, bf16[256,192]{1,0:T(8,128)(2,1)S(1)}, f32[8,512]{1,0:T(8,128)S(1)}) custom-call(bf16[1024,192]{1,0:T(8,128)(2,1)S(1)} %get-tuple-element.93.refs_0_.refs_1_, bf16[3,1024,64]{2,1,0:T(8,128)(2,1)S(1)} %get-tuple-element.90.refs_1_.refs_2_, bf16[192,1024]{1,0:T(8,128)(2,1)S(1)} %get-tuple-element.91.refs_2_), custom_call_target="tpu_custom_call" | custom-call | flops 7500000256 | bytes 1048576 | tf_op jit(solution)/shard_map/pallas_call | solution.py:163
  53.1 4.4 %collective-permute-done.15.refs_10_ = bf16[768,192]{1,0:T(8,128)(2,1)S(1)} collective-permute-done((bf16[768,192]{1,0:T(8,128)(2,1)S(1)}, bf16[768,192]{1,0:T(8,128)(2,1)S(1)}, u32[]{:S(2)}, u32[]{:S(2)}) %collective-permute-start.15) | collective-permute-done | bytes 294944 | tf_op jit(solution)/shard_map/ppermute | solution.py:30
  57.5 5.3 %shard_map.291 = (bf16[256,192]{1,0:T(8,128)(2,1)S(1)}, bf16[256,192]{1,0:T(8,128)(2,1)S(1)}, f32[8,512]{1,0:T(8,128)S(1)}) custom-call(bf16[1024,192]{1,0:T(8,128)(2,1)S(1)} %get-tuple-element.93.refs_0_.refs_1_, bf16[3,1024,64]{2,1,0:T(8,128)(2,1)S(1)} %get-tuple-element.90.refs_1_.refs_2_, bf16[192,1024]{1,0:T(8,128)(2,1)S(1)} %get-tuple-element.91.refs_2_), custom_call_target="tpu_custom_call" | custom-call | flops 7500000256 | bytes 1048576 | tf_op jit(solution)/shard_map/pallas_call | solution.py:163
  65.6 4.2 %collective-permute-done.12.refs_6_ = bf16[256,192]{1,0:T(8,128)(2,1)S(1)} collective-permute-done((bf16[256,192]{1,0:T(8,128)(2,1)S(1)}, bf16[256,192]{1,0:T(8,128)(2,1)S(1)}, u32[]{:S(2)}, u32[]{:S(2)}) %collective-permute-start.12) | collective-permute-done | bytes 98336 | tf_op jit(solution)/shard_map/ppermute | solution.py:30
  71.7 3.9 %shard_map.292 = (f32[256,768]{1,0:T(8,128)S(1)}, bf16[256,768]{1,0:T(8,128)(2,1)S(1)}, bf16[768,768]{1,0:T(8,128)(2,1)S(1)}) custom-call(s32[8]{0:T(128)S(1)} %gather_fusion, s32[4]{0:T(128)S(1)} %pad_add_fusion.refs_1_.refs_0_, f32[8,768]{1,0:T(8,128)S(1)} %get-tuple-element.88.refs_2_.refs_1_.refs_0_, bf16[256,768]{1,0:T(8,128)(2,1)S(1)} %bitcast.40, ...), custom_call_target="tpu_custom_call" | custom-call | flops 6000000000 | bytes 1048576 | tf_op jit(solution)/shard_map/pallas_call | solution.py:163
  77.8 2.3 %collective-permute-done.21.refs_4_.refs_6_ = bf16[256,768]{1,0:T(8,128)(2,1)S(1)} collective-permute-done((bf16[256,768]{1,0:T(8,128)(2,1)S(1)}, bf16[256,768]{1,0:T(8,128)(2,1)S(1)}, u32[]{:S(2)}, u32[]{:S(2)}) %collective-permute-start.21) | collective-permute-done | bytes 393248 | tf_op jit(solution)/shard_map/ppermute | solution.py:30
  85.1 6.0 %shard_map.294 = (bf16[512,768]{1,0:T(8,128)(2,1)S(1)}, bf16[512,768]{1,0:T(8,128)(2,1)S(1)}, f32[256,768]{1,0:T(8,128)S(1)}, bf16[256,768]{1,0:T(8,128)(2,1)}, ...) custom-call(s32[8]{0:T(128)S(1)} %gather_fusion, ...), custom_call_target="tpu_custom_call" | custom-call | flops 8200000000 | bytes 1048576 | tf_op jit(solution)/shard_map/pallas_call | solution.py:163
  92.3 1.7 collective-permute-done.20.refs_3_
  94.0 5.7 %shard_map.295 = (bf16[512,768]{1,0:T(8,128)(2,1)S(1)}, bf16[512,768]{1,0:T(8,128)(2,1)S(1)}, f32[256,768]{1,0:T(8,128)S(1)}, bf16[256,768]{1,0:T(8,128)(2,1)S(1...) custom-call(s32[8]{0:T(128)S(1)} %gather_fusion, ...), custom_call_target="tpu_custom_call" | custom-call | flops 8200000000 | bytes 1048576 | tf_op jit(solution)/shard_map/pallas_call | solution.py:163
  103.6 6.3 %shard_map.296 = bf16[8,192,768]{2,1,0:T(8,128)(2,1)} custom-call(bf16[256,768]{1,0:T(8,128)(2,1)S(1)} %get-tuple-element.100.refs_2_.refs_0_, bf16[256,768]{1,0:T(8,128)(2,1)S(1)} %copy-done.7, bf16[256,768]{1,0:T(8,128)(2,1)} %collective-permute-done.19.refs_2_, bf16[256,768]{1,0:T(8,128)(2,1)S(1)} %collective-permute-done.20.refs_3_, ...), custom_call_target="tpu_custom_call" | custom-call | flops 8999999488 | bytes 1048576 | tf_op jit(solution)/shard_map/pallas_call | solution.py:163
  109.9 4.0 %collective-permute-done.25.refs_6_ = bf16[256,768]{1,0:T(8,128)(2,1)} collective-permute-done((bf16[256,768]{1,0:T(8,128)(2,1)}, bf16[256,768]{1,0:T(8,128)(2,1)}, u32[]{:S(2)}, u32[]{:S(2)}) %collective-permute-start.25) | collective-permute-done | bytes 393248 | tf_op jit(solution)/shard_map/ppermute | solution.py:30
  115.1 2.8 %shard_map.297 = (f32[256,768]{1,0:T(8,128)S(1)}, bf16[256,768]{1,0:T(8,128)(2,1)S(1)}, f32[8,768]{1,0:T(8,128)S(1)}) custom-call(s32[4]{0:T(128)S(1)} %pad_add_fusion.refs_1_.refs_0_, f32[8,768]{1,0:T(8,128)S(1)} %get-tuple-element.88.refs_2_.refs_1_.refs_0_, f32[256,768]{1,0:T(8,128)S(1)} %get-tuple-element.99.refs_2_, bf16[256,768]{1,0:T(8,128)(2,1)S(1)} %bitcast.35, ...), custom_call_target="tpu_custom_call" | custom-call | flops 3000000000 | bytes 1048576 | tf_op jit(solution)/shard_map/pallas_call | solution.py:163
  122.8 1.8 shard_map.298
  124.8 8.4 %shard_map.299 = (bf16[512,192]{1,0:T(8,128)(2,1)S(1)}, f32[3,1024,64]{2,1,0:T(8,128)S(1)}, f32[3,1024,64]{2,1,0:T(8,128)S(1)}) custom-call(s32[4]{0:T(128)S(1)} %pad_add_fusion.refs_1_.refs_0_, bf16[1024,192]{1,0:T(8,128)(2,1)S(1)} %copy-done.36, bf16[3,1024,64]{2,1,0:T(8,128)(2,1)S(1)} %copy-done.30, bf16[3,1024,64]{2,1,0:T(8,128)(2,1)S(1)} %copy-done.34, ...), custom_call_target="tpu_custom_call" | custom-call | flops 12000000000 | bytes 1048576 | tf_op jit(solution)/shard_map/pallas_call | solution.py:163
  135.0 8.7 %shard_map.300.refs_1_ = bf16[1024,576]{1,0:T(8,128)(2,1)S(1)} custom-call(s32[4]{0:T(128)S(1)} %pad_add_fusion.refs_1_.refs_0_, bf16[1024,192]{1,0:T(8,128)(2,1)S(1)} %copy-done.36, bf16[3,1024,64]{2,1,0:T(8,128)(2,1)S(1)} %copy-done.30, bf16[3,1024,64]{2,1,0:T(8,128)(2,1)S(1)} %copy-done.34, bf16[192,1024]{1,0:T(8,128)(2,1)S(1)} %copy-done.38, ...), custom_call_target="tpu_custom_call" | custom-call | flops 12000000000 | bytes 1048576 | tf_op jit(solution)/shard_map/pallas_call | solution.py:163
  143.7 7.0 %shard_map.301 = (f32[4,104,768]{2,1,0:T(8,128)S(1)}, bf16[4,112,768]{2,1,0:T(8,128)(2,1)S(1)}, f32[256,768]{1,0:T(8,128)S(1)}, f32[256,768]{1,0:T(8,128)S(1)}, bf16[512,768]{1,0:T(8,128)(2,1)S(1)}) custom-call(s32[4]{0:T(128)S(1)} %pad_add_fusion.refs_1_.refs_0_, bf16[1024,576]{1,0:T(8,128)(2,1)S(1)} %shard_map.300.refs_1_, ...), custom_call_target="tpu_custom_call" | custom-call | flops 10499999744 | bytes 1048576 | tf_op jit(solution)/shard_map/pallas_call | solution.py:163
  156.4 16.5 %collective-permute-done.33.refs_2_ = bf16[4,112,768]{2,1,0:T(8,128)(2,1)S(1)} collective-permute-done((bf16[4,112,768]{2,1,0:T(8,128)(2,1)S(1)}, bf16[4,112,768]{2,1,0:T(8,128)(2,1)S(1)}, u32[]{:S(2)}, u32[]{:S(2)}) %collective-permute-start.33) | collective-permute-done | bytes 688160 | tf_op jit(solution)/shard_map/ppermute | solution.py:44
  176.9 1.8 collective-permute-start.36
  179.6 8.2 %collective-permute-done.34.refs_2_ = bf16[112,768]{1,0:T(8,128)(2,1)S(1)} collective-permute-done((bf16[112,768]{1,0:T(8,128)(2,1)S(1)}, bf16[112,768]{1,0:T(8,128)(2,1)S(1)}, u32[]{:S(2)}, u32[]{:S(2)}) %collective-permute-start.34) | collective-permute-done | bytes 172064 | tf_op jit(solution)/shard_map/ppermute | solution.py:49
  187.9 10.9 %collective-permute-done.35.refs_3_ = bf16[112,768]{1,0:T(8,128)(2,1)S(1)} collective-permute-done((bf16[112,768]{1,0:T(8,128)(2,1)S(1)}, bf16[112,768]{1,0:T(8,128)(2,1)S(1)}, u32[]{:S(2)}, u32[]{:S(2)}) %collective-permute-start.35) | collective-permute-done | bytes 172064 | tf_op jit(solution)/shard_map/ppermute | solution.py:49
  198.8 3.5 %reduce-scatter.2.cloned.1.call-done = bf16[1,192,768]{2,1,0:T(8,128)(2,1)} async-done(((bf16[8,192,768]{2,1,0:T(8,128)(2,1)}), bf16[1,192,768]{2,1,0:T(8,128)(2,1)}) %reduce-scatter.2.cloned.1.call-update) | async-done | bytes 294928 | tf_op jit(solution)/shard_map/reduce_scatter | solution.py:40
  203.3 1.8 shard_map.304
  207.7 1.9 shard_map.302
  209.7 2.4 %collective-permute-done.38.refs_3_ = bf16[304,192]{1,0:T(8,128)(2,1)S(1)} collective-permute-done((bf16[304,192]{1,0:T(8,128)(2,1)S(1)}, bf16[304,192]{1,0:T(8,128)(2,1)S(1)}, u32[]{:S(2)}, u32[]{:S(2)}) %collective-permute-start.38) | collective-permute-done | bytes 116768 | tf_op jit(solution)/shard_map/ppermute | solution.py:30
  212.1 2.5 %collective-permute-done.39.refs_4_ = bf16[304,192]{1,0:T(8,128)(2,1)S(1)} collective-permute-done((bf16[304,192]{1,0:T(8,128)(2,1)S(1)}, bf16[304,192]{1,0:T(8,128)(2,1)S(1)}, u32[]{:S(2)}, u32[]{:S(2)}) %collective-permute-start.39) | collective-permute-done | bytes 116768 | tf_op jit(solution)/shard_map/ppermute | solution.py:30
  214.6 2.4 %shard_map.305 = (f32[96,576]{1,0:T(8,128)}, f32[96,768]{1,0:T(8,128)}, f32[384,192]{1,0:T(8,128)S(1)}, f32[96,192]{1,0:T(8,128)}, f32[8,192]{1,0:T(8,128)S(1)}) custom-call(s32[4]{0:T(128)S(1)} %pad_add_fusion.refs_1_.refs_0_, bf16[304,192]{1,0:T(8,128)(2,1)S(1)} %get-tuple-element.151.refs_1_, bf16[304,192]{1,0:T(8,128)(2,1)S(1)} %collective-permute-done.37.refs_2_, ...), custom_call_target="tpu_custom_call" | custom-call | flops 3800000000 | bytes 1048576 | tf_op jit(solution)/shard_map/pallas_call | solution.py:163
  (210 shorter events, 60.1 us)
Async XLA Ops:
  7.2 75.3 %all-gather.2.cloned.1.call-start = ((), (), s32[]{:S(2)}) async-start(), calls=%async_computation.1 | async-start | bytes 2654208 | tf_op jit(solution)/shard_map/all_gather | solution.py:961
  10.4 7.2 %collective-permute-start.4 = (bf16[98,768]{1,0:T(8,128)(2,1)S(1)}, bf16[98,768]{1,0:T(8,128)(2,1)S(1)}, u32[]{:S(2)}, u32[]{:S(2)}) collective-permute-start(bf16[98,768]{1,0:T(8,128)(2,1)S(1)} %pad_maximum_fusion.refs_6_), channel_id=1, source_target_pairs={{8,0},{16,8},{24,16},{28,24},{20,28},{12,20},{4,12},{0,4},{9,1},{1... | collective-permute-start | bytes 451592 | tf_op jit(solution)/shard_map/ppermute | solution.py:73
  13.4 5.6 %collective-permute-start.3 = (bf16[98,768]{1,0:T(8,128)(2,1)S(1)}, bf16[98,768]{1,0:T(8,128)(2,1)S(1)}, u32[]{:S(2)}, u32[]{:S(2)}) collective-permute-start(bf16[98,768]{1,0:T(8,128)(2,1)S(1)} %pad_maximum_fusion.refs_6_), channel_id=1, source_target_pairs={{0,8},{8,16},{16,24},{24,28},{28,20},{20,12},{12,4},{4,0},{1,9},{9... | collective-permute-start | bytes 451592 | tf_op jit(solution)/shard_map/ppermute | solution.py:72
  20.6 181.7 %reduce-scatter.2.cloned.1.call-start = ((), (), s32[]{:S(2)}) async-start(), calls=%async_computation.2 | async-start | bytes 2654208 | tf_op jit(solution)/shard_map/reduce_scatter | solution.py:40
  22.8 18.1 %collective-permute-start = (bf16[256,768]{1,0:T(8,128)(2,1)S(1)}, bf16[256,768]{1,0:T(8,128)(2,1)S(1)}, u32[]{:S(2)}, u32[]{:S(2)}) collective-permute-start(bf16[256,768]{1,0:T(8,128)(2,1)S(1)} %bitcast.36), channel_id=1, source_target_pairs={{0,1},{1,0},{2,3},{3,2},{4,5},{5,4},{6,7},{7,6},{8,9},{9,8},{10,11... | collective-permute-start | bytes 1179656 | tf_op jit(solution)/shard_map/ppermute | solution.py:30
  22.8 18.1 %collective-permute-start.1 = (bf16[256,768]{1,0:T(8,128)(2,1)S(1)}, bf16[256,768]{1,0:T(8,128)(2,1)S(1)}, u32[]{:S(2)}, u32[]{:S(2)}) collective-permute-start(bf16[256,768]{1,0:T(8,128)(2,1)S(1)} %bitcast.37), channel_id=1, source_target_pairs={{0,2},{1,3},{2,0},{3,1},{4,6},{5,7},{6,4},{7,5},{8,10},{9,11},{10,... | collective-permute-start | bytes 1179656 | tf_op jit(solution)/shard_map/ppermute | solution.py:30
  24.3 18.0 %collective-permute-start.2 = (bf16[256,768]{1,0:T(8,128)(2,1)S(1)}, bf16[256,768]{1,0:T(8,128)(2,1)S(1)}, u32[]{:S(2)}, u32[]{:S(2)}) collective-permute-start(bf16[256,768]{1,0:T(8,128)(2,1)S(1)} %bitcast.38), channel_id=1, source_target_pairs={{0,3},{1,2},{2,1},{3,0},{4,7},{5,6},{6,5},{7,4},{8,11},{9,10},{10,... | collective-permute-start | bytes 1179656 | tf_op jit(solution)/shard_map/ppermute | solution.py:30
  26.0 6.8 %collective-permute-start.8 = (bf16[98,768]{1,0:T(8,128)(2,1)S(1)}, bf16[98,768]{1,0:T(8,128)(2,1)S(1)}, u32[]{:S(2)}, u32[]{:S(2)}) collective-permute-start(bf16[98,768]{1,0:T(8,128)(2,1)S(1)} %collective-permute-done.6.refs_10_), channel_id=1, source_target_pairs={{8,0},{16,8},{24,16},{28,24},{20,28},{12,20},{4,12},{0,4},{9,1},{1... | collective-permute-start | bytes 451592 | tf_op jit(solution)/shard_map/ppermute | solution.py:73
  27.6 7.8 %collective-permute-start.7 = (bf16[98,768]{1,0:T(8,128)(2,1)S(1)}, bf16[98,768]{1,0:T(8,128)(2,1)S(1)}, u32[]{:S(2)}, u32[]{:S(2)}) collective-permute-start(bf16[98,768]{1,0:T(8,128)(2,1)S(1)} %collective-permute-done.5.refs_9_), channel_id=1, source_target_pairs={{0,8},{8,16},{16,24},{24,28},{28,20},{20,12},{12,4},{4,0},{1,9},{9... | collective-permute-start | bytes 451592 | tf_op jit(solution)/shard_map/ppermute | solution.py:72
  32.9 8.0 %collective-permute-start.10 = (bf16[50,768]{1,0:T(8,128)(2,1)S(1)}, bf16[50,768]{1,0:T(8,128)(2,1)S(1)}, u32[]{:S(2)}, u32[]{:S(2)}) collective-permute-start(bf16[50,768]{1,0:T(8,128)(2,1)S(1)} %slice.64), channel_id=1, source_target_pairs={{8,0},{16,8},{24,16},{28,24},{20,28},{12,20},{4,12},{0,4},{9,1},{1... | collective-permute-start | bytes 230408 | tf_op jit(solution)/shard_map/ppermute | solution.py:76
  45.8 11.7 %collective-permute-start.15 = (bf16[768,192]{1,0:T(8,128)(2,1)S(1)}, bf16[768,192]{1,0:T(8,128)(2,1)S(1)}, u32[]{:S(2)}, u32[]{:S(2)}) collective-permute-start(bf16[768,192]{1,0:T(8,128)(2,1)S(1)} %get-tuple-element.97.refs_8_), channel_id=1, source_target_pairs={{0,2},{1,3},{2,0},{3,1},{4,6},{5,7},{6,4},{7,5},{8,10},{9,11},{10,... | collective-permute-start | bytes 884744 | tf_op jit(solution)/shard_map/ppermute | solution.py:30
  47.4 24.2 %collective-permute-start.14 = (bf16[768,192]{1,0:T(8,128)(2,1)S(1)}, bf16[768,192]{1,0:T(8,128)(2,1)S(1)}, u32[]{:S(2)}, u32[]{:S(2)}) collective-permute-start(bf16[768,192]{1,0:T(8,128)(2,1)S(1)} %get-tuple-element.97.refs_8_), channel_id=1, source_target_pairs={{0,1},{1,0},{2,3},{3,2},{4,5},{5,4},{6,7},{7,6},{8,9},{9,8},{10,11... | collective-permute-start | bytes 884744 | tf_op jit(solution)/shard_map/ppermute | solution.py:30
  57.5 14.1 %collective-permute-start.16 = (bf16[768,192]{1,0:T(8,128)(2,1)S(1)}, bf16[768,192]{1,0:T(8,128)(2,1)S(1)}, u32[]{:S(2)}, u32[]{:S(2)}) collective-permute-start(bf16[768,192]{1,0:T(8,128)(2,1)S(1)} %collective-permute-done.15.refs_10_), channel_id=1, source_target_pairs={{0,1},{1,0},{2,3},{3,2},{4,5},{5,4},{6,7},{7,6},{8,9},{9,8},{10,11... | collective-permute-start | bytes 884744 | tf_op jit(solution)/shard_map/ppermute | solution.py:30
  63.5 6.4 %collective-permute-start.12 = (bf16[256,192]{1,0:T(8,128)(2,1)S(1)}, bf16[256,192]{1,0:T(8,128)(2,1)S(1)}, u32[]{:S(2)}, u32[]{:S(2)}) collective-permute-start(bf16[256,192]{1,0:T(8,128)(2,1)S(1)} %get-tuple-element.92.refs_7_), channel_id=1, source_target_pairs={{0,2},{1,3},{2,0},{3,1},{4,6},{5,7},{6,4},{7,5},{8,10},{9,11},{10,... | collective-permute-start | bytes 294920 | tf_op jit(solution)/shard_map/ppermute | solution.py:30
  65.0 6.7 %collective-permute-start.13 = (bf16[256,192]{1,0:T(8,128)(2,1)S(1)}, bf16[256,192]{1,0:T(8,128)(2,1)S(1)}, u32[]{:S(2)}, u32[]{:S(2)}) collective-permute-start(bf16[256,192]{1,0:T(8,128)(2,1)S(1)} %get-tuple-element.96.refs_8_), channel_id=1, source_target_pairs={{0,3},{1,2},{2,1},{3,0},{4,7},{5,6},{6,5},{7,4},{8,11},{9,10},{10,... | collective-permute-start | bytes 294920 | tf_op jit(solution)/shard_map/ppermute | solution.py:30
  65.0 16.7 %collective-permute-start.18 = (bf16[256,768]{1,0:T(8,128)(2,1)S(1)}, bf16[256,768]{1,0:T(8,128)(2,1)S(1)}, u32[]{:S(2)}, u32[]{:S(2)}) collective-permute-start(bf16[256,768]{1,0:T(8,128)(2,1)S(1)} %bitcast.31), channel_id=1, source_target_pairs={{0,1},{1,0},{2,3},{3,2},{4,5},{5,4},{6,7},{7,6},{8,9},{9,8},{10,11... | collective-permute-start | bytes 1179656 | tf_op jit(solution)/shard_map/ppermute | solution.py:30
  69.8 10.4 %collective-permute-start.21 = (bf16[256,768]{1,0:T(8,128)(2,1)S(1)}, bf16[256,768]{1,0:T(8,128)(2,1)S(1)}, u32[]{:S(2)}, u32[]{:S(2)}) collective-permute-start(bf16[256,768]{1,0:T(8,128)(2,1)S(1)} %bitcast.32), channel_id=1, source_target_pairs={{0,2},{1,3},{2,0},{3,1},{4,6},{5,7},{6,4},{7,5},{8,10},{9,11},{10,... | collective-permute-start | bytes 1179656 | tf_op jit(solution)/shard_map/ppermute | solution.py:30
  80.2 12.1 %collective-permute-start.22 = (bf16[256,768]{1,0:T(8,128)(2,1)S(1)}, bf16[256,768]{1,0:T(8,128)(2,1)}, u32[]{:S(2)}, u32[]{:S(2)}) collective-permute-start(bf16[256,768]{1,0:T(8,128)(2,1)S(1)} %collective-permute-done.21.refs_4_.refs_6_), channel_id=1, source_target_pairs={{0,1},{1,0},{2,3},{3,2},{4,5},{5,4},{6,7},{7,6},{8,9},{9,8},{10,11... | collective-permute-start | bytes 1179656 | tf_op jit(solution)/shard_map/ppermute | solution.py:30
  80.2 11.9 %collective-permute-start.19 = (bf16[256,768]{1,0:T(8,128)(2,1)S(1)}, bf16[256,768]{1,0:T(8,128)(2,1)}, u32[]{:S(2)}, u32[]{:S(2)}) collective-permute-start(bf16[256,768]{1,0:T(8,128)(2,1)S(1)} %get-tuple-element.100.refs_2_.refs_0_), channel_id=1, source_target_pairs={{0,2},{1,3},{2,0},{3,1},{4,6},{5,7},{6,4},{7,5},{8,10},{9,11},{10,... | collective-permute-start | bytes 1179656 | tf_op jit(solution)/shard_map/ppermute | solution.py:30
  100.0 13.9 %collective-permute-start.23 = (bf16[256,768]{1,0:T(8,128)(2,1)}, bf16[256,768]{1,0:T(8,128)(2,1)}, u32[]{:S(2)}, u32[]{:S(2)}) collective-permute-start(bf16[256,768]{1,0:T(8,128)(2,1)} %get-tuple-element.109), channel_id=1, source_target_pairs={{0,1},{1,0},{2,3},{3,2},{4,5},{5,4},{6,7},{7,6},{8,9},{9,8},{10,11... | collective-permute-start | bytes 1179656 | tf_op jit(solution)/shard_map/ppermute | solution.py:30
  102.4 11.6 %collective-permute-start.25 = (bf16[256,768]{1,0:T(8,128)(2,1)}, bf16[256,768]{1,0:T(8,128)(2,1)}, u32[]{:S(2)}, u32[]{:S(2)}) collective-permute-start(bf16[256,768]{1,0:T(8,128)(2,1)} %add_convert_fusion.3), channel_id=1, source_target_pairs={{0,2},{1,3},{2,0},{3,1},{4,6},{5,7},{6,4},{7,5},{8,10},{9,11},{10,... | collective-permute-start | bytes 1179656 | tf_op jit(solution)/shard_map/ppermute | solution.py:30
  117.9 6.7 %collective-permute-start.26 = (bf16[256,768]{1,0:T(8,128)(2,1)S(1)}, bf16[256,768]{1,0:T(8,128)(2,1)S(1)}, u32[]{:S(2)}, u32[]{:S(2)}) collective-permute-start(bf16[256,768]{1,0:T(8,128)(2,1)S(1)} %get-tuple-element.116.refs_6_.refs_9_), channel_id=1, source_target_pairs={{0,1},{1,0},{2,3},{3,2},{4,5},{5,4},{6,7},{7,6},{8,9},{9,8},{10,11... | collective-permute-start | bytes 1179656 | tf_op jit(solution)/shard_map/ppermute | solution.py:30
  118.0 15.2 %collective-permute-start.29 = (bf16[256,768]{1,0:T(8,128)(2,1)S(1)}, bf16[256,768]{1,0:T(8,128)(2,1)S(1)}, u32[]{:S(2)}, u32[]{:S(2)}) collective-permute-start(bf16[256,768]{1,0:T(8,128)(2,1)S(1)} %get-tuple-element.116.refs_6_.refs_9_), channel_id=1, source_target_pairs={{0,2},{1,3},{2,0},{3,1},{4,6},{5,7},{6,4},{7,5},{8,10},{9,11},{10,... | collective-permute-start | bytes 1179656 | tf_op jit(solution)/shard_map/ppermute | solution.py:30
  133.5 19.9 %collective-permute-start.27 = (bf16[512,768]{1,0:T(8,128)(2,1)S(1)}, bf16[512,768]{1,0:T(8,128)(2,1)S(1)}, u32[]{:S(2)}, u32[]{:S(2)}) collective-permute-start(bf16[512,768]{1,0:T(8,128)(2,1)S(1)} %get-tuple-element.126), channel_id=1, source_target_pairs={{0,1},{1,0},{2,3},{3,2},{4,5},{5,4},{6,7},{7,6},{8,9},{9,8},{10,11... | collective-permute-start | bytes 2359304 | tf_op jit(solution)/shard_map/ppermute | solution.py:30
  151.8 21.2 %collective-permute-start.33 = (bf16[4,112,768]{2,1,0:T(8,128)(2,1)S(1)}, bf16[4,112,768]{2,1,0:T(8,128)(2,1)S(1)}, u32[]{:S(2)}, u32[]{:S(2)}) collective-permute-start(bf16[4,112,768]{2,1,0:T(8,128)(2,1)S(1)} %get-tuple-element.145), channel_id=1, source_target_pairs={{0,4},{4,0},{8,12},{12,8},{16,20},{20,16},{24,28},{28,24},{1,5},{5... | collective-permute-start | bytes 2064392 | tf_op jit(solution)/shard_map/ppermute | solution.py:44
  153.5 25.2 %collective-permute-start.28 = (bf16[256,768]{1,0:T(8,128)(2,1)S(1)}, bf16[256,768]{1,0:T(8,128)(2,1)S(1)}, u32[]{:S(2)}, u32[]{:S(2)}) collective-permute-start(bf16[256,768]{1,0:T(8,128)(2,1)S(1)} %add_convert_fusion.2), channel_id=1, source_target_pairs={{0,2},{1,3},{2,0},{3,1},{4,6},{5,7},{6,4},{7,5},{8,10},{9,11},{10,... | collective-permute-start | bytes 1179656 | tf_op jit(solution)/shard_map/ppermute | solution.py:30
  155.2 52.5 %collective-permute-start.32 = (bf16[256,768]{1,0:T(8,128)(2,1)}, bf16[256,768]{1,0:T(8,128)(2,1)S(1)}, u32[]{:S(2)}, u32[]{:S(2)}) collective-permute-start(bf16[256,768]{1,0:T(8,128)(2,1)} %add_convert_fusion), channel_id=1, source_target_pairs={{0,2},{1,3},{2,0},{3,1},{4,6},{5,7},{6,4},{7,5},{8,10},{9,11},{10,... | collective-permute-start | bytes 1179656 | tf_op jit(solution)/shard_map/ppermute | solution.py:30
  174.2 13.6 %collective-permute-start.34 = (bf16[112,768]{1,0:T(8,128)(2,1)S(1)}, bf16[112,768]{1,0:T(8,128)(2,1)S(1)}, u32[]{:S(2)}, u32[]{:S(2)}) collective-permute-start(bf16[112,768]{1,0:T(8,128)(2,1)S(1)} %get-tuple-element.148), channel_id=1, source_target_pairs={{0,8},{4,12},{8,0},{12,4},{16,24},{20,28},{24,16},{28,20},{1,9},{5... | collective-permute-start | bytes 516104 | tf_op jit(solution)/shard_map/ppermute | solution.py:49
  175.4 23.4 %collective-permute-start.35 = (bf16[112,768]{1,0:T(8,128)(2,1)S(1)}, bf16[112,768]{1,0:T(8,128)(2,1)S(1)}, u32[]{:S(2)}, u32[]{:S(2)}) collective-permute-start(bf16[112,768]{1,0:T(8,128)(2,1)S(1)} %get-tuple-element.149), channel_id=1, source_target_pairs={{0,16},{4,20},{8,24},{12,28},{16,0},{20,4},{24,8},{28,12},{1,17},{... | collective-permute-start | bytes 516104 | tf_op jit(solution)/shard_map/ppermute | solution.py:49
  176.9 21.9 %collective-permute-start.36 = (bf16[112,768]{1,0:T(8,128)(2,1)S(1)}, bf16[112,768]{1,0:T(8,128)(2,1)S(1)}, u32[]{:S(2)}, u32[]{:S(2)}) collective-permute-start(bf16[112,768]{1,0:T(8,128)(2,1)S(1)} %get-tuple-element.150), channel_id=1, source_target_pairs={{0,24},{4,28},{8,16},{12,20},{16,8},{20,12},{24,0},{28,4},{1,25},{... | collective-permute-start | bytes 516104 | tf_op jit(solution)/shard_map/ppermute | solution.py:49
  205.3 6.8 %collective-permute-start.38 = (bf16[304,192]{1,0:T(8,128)(2,1)S(1)}, bf16[304,192]{1,0:T(8,128)(2,1)S(1)}, u32[]{:S(2)}, u32[]{:S(2)}) collective-permute-start(bf16[304,192]{1,0:T(8,128)(2,1)S(1)} %get-tuple-element.153), channel_id=1, source_target_pairs={{0,2},{1,3},{2,0},{3,1},{4,6},{5,7},{6,4},{7,5},{8,10},{9,11},{10,... | collective-permute-start | bytes 350216 | tf_op jit(solution)/shard_map/ppermute | solution.py:30
  206.4 8.3 %collective-permute-start.39 = (bf16[304,192]{1,0:T(8,128)(2,1)S(1)}, bf16[304,192]{1,0:T(8,128)(2,1)S(1)}, u32[]{:S(2)}, u32[]{:S(2)}) collective-permute-start(bf16[304,192]{1,0:T(8,128)(2,1)S(1)} %get-tuple-element.154), channel_id=1, source_target_pairs={{0,3},{1,2},{2,1},{3,0},{4,7},{5,6},{6,5},{7,4},{8,11},{9,10},{10,... | collective-permute-start | bytes 350216 | tf_op jit(solution)/shard_map/ppermute | solution.py:30
  (65 other events, 348.4 us)
Sparse Core Ops, SparseCore 0:
  20.8 53.8 all-gather.1
  118.1 84.1 reduce-scatter.1
where the time goes:
time: 230 us; the launch traced here: 226 us
  waiting for transfers between devices  79.5 us (35%)
  Pallas kernels  73.7 us (32%)
  starting transfers between devices  36.1 us (16%)
  local copies, waits for them, and re-layouts  18.4 us (8%)
  between operations  15.1 us (7%)
  other arithmetic  3.52 us (2%)
    pallas_call x16, Pallas kernels, run(): pl.pallas_call(wrapped, out_shape=tuple(out_shape), in_specs=[SMEM] * n_s...  70.2 us
    ppermute x28, waiting for transfers between devices, seq_swap(): return lax.ppermute(value, 'seq', [(i, i ^ step) for i in range(GROUPS)])  25.8 us
    ppermute x3, waiting for transfers between devices, plane_swaps(): lax.ppermute(part, 'fsdp', [(i, i ^ 2 * step) for i in range(count)])  19.2 us
    ppermute x28, starting transfers between devices, seq_swap(): return lax.ppermute(value, 'seq', [(i, i ^ step) for i in range(GROUPS)])  19 us
    ppermute x1, waiting for transfers between devices, side_swap(): return lax.ppermute(value, 'fsdp', [(i, i ^ 1) for i in range(count)])  16.5 us
    unnamed x111, local copies, waits for them, and re-layouts  13.3 us
    ppermute x3, waiting for transfers between devices, ring_gather(): right = lax.ppermute(right, 'fsdp', back)  8.89 us
    ppermute x3, starting transfers between devices, ring_gather(): right = lax.ppermute(right, 'fsdp', back)  6.2 us
  transfers between devices with their start and end apart: 43, of which 20 were waited for; matrix products, arithmetic and copies ran while one was open for 2% of the time, Pallas kernels for 27%

commit v1 on v0

--- a/solution.py
+++ b/solution.py
@@ -1001,9 +1001,9 @@
     o2, o3, lse_b = attend(1, queries, keys, v_turned)
     far2, far3 = seq_swap(o2, 2), seq_swap(o3, 3)
     queries_a = after(queries, o2)
+    o0, o1, lse_a = attend(0, queries_a, keys, v_turned)
     if ring:
-        out_blocks.append(seq_swap(after(out_blocks[2], o2), 1))
-    o0, o1, lse_a = attend(0, queries_a, keys, v_turned)
+        out_blocks.append(seq_swap(after(out_blocks[2], o0), 1))
     o_pieces = [o0, seq_swap(o1, 1), far2, far3]
     pieces = seq_pieces(after(dy, o0))
     h, act2, w_out = mix(where, me, vec, x, o_pieces, out_blocks, own, group)
@@ -1026,17 +1026,12 @@
     far = after(far, feed_parts)
     dh, db, sums2 = turn(me, vec, h, dy, part0, near0, far)
     db_pieces = [db, seq_swap(db, 1), seq_swap(db, 2)]
-    y_parts = feed_out((g_a, after(g_b, db)), w_down)
-    lse_a = after(lse_a, y_parts[0])
     back_a = back_first(me, queries, keys, values, k_turned, lse_a, db_pieces[:2], w_out)
     db_pieces.append(seq_swap(after(db_pieces[2], back_a[0]), 1))
-    y_near = seq_swap(after(y_parts[2], back_a[0]), 1)
-    y_sum = (y_parts[1] + y_near[rows:].astype(F32)).astype(BF)
     lse_b = after(lse_b, back_a[0])
     dqkv = back_second(
         me, queries, keys, values, k_turned, lse_b, w_out, back_a, db_pieces[2:]
     )
-    y_far = seq_swap(after(y_sum, back_a[0]), 2)
     os = (o0, o1, o2, o3)
     closed = close(
         me, dqkv, act1, w_qkv, x_kept, os, db_pieces, sums2, usum_a, usum_b, own, planes
@@ -1047,12 +1042,16 @@
     else:
         grad_heads, part0, part2, sent, sums1 = closed
     near = seq_swap(sent, 1)
+    y_parts = feed_out((g_a, after(g_b, sent)), w_down)
+    y_near = seq_swap(y_parts[2], 1)
+    y_sum = (y_parts[1] + y_near[rows:].astype(F32)).astype(BF)
     far_sum = (part2 + near[rows:].astype(F32)).astype(BF)
     if ring:
         got = after(got, far_sum)
         own_sum, *sends = plane_parts(me, keep, got)
         arrived = plane_swaps(sends, count)
     far1 = seq_swap(far_sum, 2)
+    y_far = seq_swap(after(y_sum, far_sum), 2)
     layer_out = h + (y_parts[0] + y_near[:rows].astype(F32) + y_far.astype(F32)) + vec[6]
     layer_out = layer_out.astype(BF).reshape(frames_in.shape)
     input_grad = finish(vec, x, dh, part0, near, far1).reshape(frames_in.shape)

time: 230 us -> 226 us (0.983)
  waiting for transfers between devices: 79.5 us -> 75.3 us
    ppermute x28, starting transfers between devices: 19 us -> 16.3 us  [seq_swap(): return lax.ppermute(value, 'seq', [(i, i ^ step) for i in range(GROUPS)])]
    ppermute x1, starting transfers between devices: 1.58 us -> 4.09 us  [side_swap(): return lax.ppermute(value, 'fsdp', [(i, i ^ 1) for i in range(count)])]
    unnamed x111 -> x121, local copies, waits for them, and re-layouts: 13.3 us -> 13.3 us
  transfers between devices with their start and end apart: 43 -> 43, of which waited for: 20 -> 22; matrix products, arithmetic and copies ran while one was open for 2% -> 2% of each run, Pallas kernels for 27% -> 28%
where the time goes in v1:
time: 226 us; the launch traced here: 222 us
  waiting for transfers between devices  75.3 us (33%)
  Pallas kernels  73.9 us (33%)
  starting transfers between devices  35.8 us (16%)
  local copies, waits for them, and re-layouts  18.4 us (8%)
  between operations  15.2 us (7%)
  other arithmetic  3.53 us (2%)
    pallas_call x16, Pallas kernels, run(): pl.pallas_call(wrapped, out_shape=tuple(out_shape), in_specs=[SMEM] * n_s...  70.5 us
    ppermute x28, waiting for transfers between devices, seq_swap(): return lax.ppermute(value, 'seq', [(i, i ^ step) for i in range(GROUPS)])  25.3 us
    ppermute x3, waiting for transfers between devices, plane_swaps(): lax.ppermute(part, 'fsdp', [(i, i ^ 2 * step) for i in range(count)])  18.3 us
    ppermute x28, starting transfers between devices, seq_swap(): return lax.ppermute(value, 'seq', [(i, i ^ step) for i in range(GROUPS)])  16.3 us
    ppermute x1, waiting for transfers between devices, side_swap(): return lax.ppermute(value, 'fsdp', [(i, i ^ 1) for i in range(count)])  14.8 us
    unnamed x121, local copies, waits for them, and re-layouts  13.3 us
    ppermute x3, waiting for transfers between devices, ring_gather(): right = lax.ppermute(right, 'fsdp', back)  8.89 us
    ppermute x3, starting transfers between devices, ring_gather(): right = lax.ppermute(right, 'fsdp', back)  6.2 us
  transfers between devices with their start and end apart: 43, of which 22 were waited for; matrix products, arithmetic and copies ran while one was open for 2% of the time, Pallas kernels for 28%

profile of v1, /device:TPU:0, one launch (start us, length us, event | category | flops | bytes accessed | tf_op | source)
XLA Modules:
  0.0 222.1 jit_solution(14571607753136914623)
XLA Ops:
  10.4 3.0 %collective-permute-start.4 = (bf16[98,768]{1,0:T(8,128)(2,1)S(1)}, bf16[98,768]{1,0:T(8,128)(2,1)S(1)}, u32[]{:S(2)}, u32[]{:S(2)}) collective-permute-start(bf16[98,768]{1,0:T(8,128)(2,1)S(1)} %pad_maximum_fusion.refs_6_), channel_id=1, source_target_pairs={{8,0},{16,8},{24,16},{28,24},{20,28},{12,20},{4,12},{0,4},{9,1},{1... | collective-permute-start | bytes 451592 | tf_op jit(solution)/shard_map/ppermute | solution.py:73
  13.6 4.0 %collective-permute-done.4.refs_8_ = bf16[98,768]{1,0:T(8,128)(2,1)S(1)} collective-permute-done((bf16[98,768]{1,0:T(8,128)(2,1)S(1)}, bf16[98,768]{1,0:T(8,128)(2,1)S(1)}, u32[]{:S(2)}, u32[]{:S(2)}) %collective-permute-start.4) | collective-permute-done | bytes 150560 | tf_op jit(solution)/shard_map/ppermute | solution.py:73
  28.7 4.1 %collective-permute-done.8.refs_12_ = bf16[98,768]{1,0:T(8,128)(2,1)S(1)} collective-permute-done((bf16[98,768]{1,0:T(8,128)(2,1)S(1)}, bf16[98,768]{1,0:T(8,128)(2,1)S(1)}, u32[]{:S(2)}, u32[]{:S(2)}) %collective-permute-start.8) | collective-permute-done | bytes 150560 | tf_op jit(solution)/shard_map/ppermute | solution.py:73
  32.9 2.5 %collective-permute-start.10 = (bf16[50,768]{1,0:T(8,128)(2,1)S(1)}, bf16[50,768]{1,0:T(8,128)(2,1)S(1)}, u32[]{:S(2)}, u32[]{:S(2)}) collective-permute-start(bf16[50,768]{1,0:T(8,128)(2,1)S(1)} %slice.64), channel_id=1, source_target_pairs={{8,0},{16,8},{24,16},{28,24},{20,28},{12,20},{4,12},{0,4},{9,1},{1... | collective-permute-start | bytes 230408 | tf_op jit(solution)/shard_map/ppermute | solution.py:76
  36.6 4.2 %collective-permute-done.9 = bf16[48,768]{1,0:T(8,128)(2,1)S(1)} collective-permute-done((bf16[48,768]{1,0:T(8,128)(2,1)S(1)}, bf16[48,768]{1,0:T(8,128)(2,1)S(1)}, u32[]{:S(2)}, u32[]{:S(2)}) %collective-permute-start.9) | collective-permute-done | bytes 73760 | tf_op jit(solution)/shard_map/ppermute | solution.py:76
  42.3 3.4 %shard_map.289 = (bf16[1024,768]{1,0:T(8,128)(2,1)S(1)}, bf16[1024,192]{1,0:T(8,128)(2,1)S(1)}, bf16[3,1024,64]{2,1,0:T(8,128)(2,1)S(1)}, bf16[3,1024,64]{2,1,0:...) custom-call(s32[8]{0:T(128)S(1)} %gather_fusion, ...), custom_call_target="tpu_custom_call" | custom-call | flops 8999999488 | bytes 1048576 | tf_op jit(solution)/shard_map/pallas_call | solution.py:139
  47.8 5.3 %shard_map.290 = (bf16[256,192]{1,0:T(8,128)(2,1)S(1)}, bf16[256,192]{1,0:T(8,128)(2,1)S(1)}, f32[8,512]{1,0:T(8,128)S(1)}) custom-call(bf16[1024,192]{1,0:T(8,128)(2,1)S(1)} %get-tuple-element.91.refs_0_.refs_1_, bf16[3,1024,64]{2,1,0:T(8,128)(2,1)S(1)} %get-tuple-element.88.refs_1_.refs_2_, bf16[192,1024]{1,0:T(8,128)(2,1)S(1)} %get-tuple-element.89.refs_2_), custom_call_target="tpu_custom_call" | custom-call | flops 7500000256 | bytes 1048576 | tf_op jit(solution)/shard_map/pallas_call | solution.py:163
  53.2 5.3 %shard_map.291 = (bf16[256,192]{1,0:T(8,128)(2,1)S(1)}, bf16[256,192]{1,0:T(8,128)(2,1)S(1)}, f32[8,512]{1,0:T(8,128)S(1)}) custom-call(bf16[1024,192]{1,0:T(8,128)(2,1)S(1)} %get-tuple-element.91.refs_0_.refs_1_, bf16[3,1024,64]{2,1,0:T(8,128)(2,1)S(1)} %get-tuple-element.88.refs_1_.refs_2_, bf16[192,1024]{1,0:T(8,128)(2,1)S(1)} %get-tuple-element.89.refs_2_), custom_call_target="tpu_custom_call" | custom-call | flops 7500000256 | bytes 1048576 | tf_op jit(solution)/shard_map/pallas_call | solution.py:163
  61.2 4.2 %collective-permute-done.12.refs_6_ = bf16[256,192]{1,0:T(8,128)(2,1)S(1)} collective-permute-done((bf16[256,192]{1,0:T(8,128)(2,1)S(1)}, bf16[256,192]{1,0:T(8,128)(2,1)S(1)}, u32[]{:S(2)}, u32[]{:S(2)}) %collective-permute-start.12) | collective-permute-done | bytes 98336 | tf_op jit(solution)/shard_map/ppermute | solution.py:30
  66.8 3.9 %shard_map.292 = (f32[256,768]{1,0:T(8,128)S(1)}, bf16[256,768]{1,0:T(8,128)(2,1)S(1)}, bf16[768,768]{1,0:T(8,128)(2,1)S(1)}) custom-call(s32[8]{0:T(128)S(1)} %gather_fusion, s32[4]{0:T(128)S(1)} %pad_add_fusion.refs_1_.refs_0_, f32[8,768]{1,0:T(8,128)S(1)} %get-tuple-element.86.refs_2_.refs_1_.refs_0_, bf16[256,768]{1,0:T(8,128)(2,1)S(1)} %bitcast.40, ...), custom_call_target="tpu_custom_call" | custom-call | flops 6000000000 | bytes 1048576 | tf_op jit(solution)/shard_map/pallas_call | solution.py:163
  73.4 2.5 %collective-permute-done.21.refs_4_.refs_6_ = bf16[256,768]{1,0:T(8,128)(2,1)S(1)} collective-permute-done((bf16[256,768]{1,0:T(8,128)(2,1)S(1)}, bf16[256,768]{1,0:T(8,128)(2,1)S(1)}, u32[]{:S(2)}, u32[]{:S(2)}) %collective-permute-start.21) | collective-permute-done | bytes 393248 | tf_op jit(solution)/shard_map/ppermute | solution.py:30
  79.8 6.0 %shard_map.294 = (bf16[512,768]{1,0:T(8,128)(2,1)S(1)}, bf16[512,768]{1,0:T(8,128)(2,1)S(1)}, f32[256,768]{1,0:T(8,128)S(1)}, bf16[256,768]{1,0:T(8,128)(2,1)}, ...) custom-call(s32[8]{0:T(128)S(1)} %gather_fusion, ...), custom_call_target="tpu_custom_call" | custom-call | flops 8200000000 | bytes 1048576 | tf_op jit(solution)/shard_map/pallas_call | solution.py:163
  87.6 1.9 collective-permute-done.20.refs_3_
  89.5 5.7 %shard_map.295 = (bf16[512,768]{1,0:T(8,128)(2,1)S(1)}, bf16[512,768]{1,0:T(8,128)(2,1)S(1)}, f32[256,768]{1,0:T(8,128)S(1)}, bf16[256,768]{1,0:T(8,128)(2,1)S(1...) custom-call(s32[8]{0:T(128)S(1)} %gather_fusion, ...), custom_call_target="tpu_custom_call" | custom-call | flops 8200000000 | bytes 1048576 | tf_op jit(solution)/shard_map/pallas_call | solution.py:163
  98.5 6.3 %shard_map.296 = bf16[8,192,768]{2,1,0:T(8,128)(2,1)} custom-call(bf16[256,768]{1,0:T(8,128)(2,1)S(1)} %get-tuple-element.98.refs_2_.refs_0_, bf16[256,768]{1,0:T(8,128)(2,1)S(1)} %copy-done.7, bf16[256,768]{1,0:T(8,128)(2,1)} %collective-permute-done.19.refs_2_, bf16[256,768]{1,0:T(8,128)(2,1)S(1)} %collective-permute-done.20.refs_3_, ...), custom_call_target="tpu_custom_call" | custom-call | flops 8999999488 | bytes 1048576 | tf_op jit(solution)/shard_map/pallas_call | solution.py:163
  104.9 4.5 %collective-permute-done.25.refs_6_ = bf16[256,768]{1,0:T(8,128)(2,1)} collective-permute-done((bf16[256,768]{1,0:T(8,128)(2,1)}, bf16[256,768]{1,0:T(8,128)(2,1)}, u32[]{:S(2)}, u32[]{:S(2)}) %collective-permute-start.25) | collective-permute-done | bytes 393248 | tf_op jit(solution)/shard_map/ppermute | solution.py:30
  110.5 2.8 %shard_map.297 = (f32[256,768]{1,0:T(8,128)S(1)}, bf16[256,768]{1,0:T(8,128)(2,1)S(1)}, f32[8,768]{1,0:T(8,128)S(1)}) custom-call(s32[4]{0:T(128)S(1)} %pad_add_fusion.refs_1_.refs_0_, f32[8,768]{1,0:T(8,128)S(1)} %get-tuple-element.86.refs_2_.refs_1_.refs_0_, f32[256,768]{1,0:T(8,128)S(1)} %get-tuple-element.97.refs_2_, bf16[256,768]{1,0:T(8,128)(2,1)S(1)} %bitcast.35, ...), custom_call_target="tpu_custom_call" | custom-call | flops 3000000000 | bytes 1048576 | tf_op jit(solution)/shard_map/pallas_call | solution.py:163
  119.7 8.4 %shard_map.298 = (bf16[512,192]{1,0:T(8,128)(2,1)S(1)}, f32[3,1024,64]{2,1,0:T(8,128)S(1)}, f32[3,1024,64]{2,1,0:T(8,128)S(1)}) custom-call(s32[4]{0:T(128)S(1)} %pad_add_fusion.refs_1_.refs_0_, bf16[1024,192]{1,0:T(8,128)(2,1)S(1)} %copy-done.39, bf16[3,1024,64]{2,1,0:T(8,128)(2,1)S(1)} %copy-done.31, bf16[3,1024,64]{2,1,0:T(8,128)(2,1)S(1)} %copy-done.36, ...), custom_call_target="tpu_custom_call" | custom-call | flops 12000000000 | bytes 1048576 | tf_op jit(solution)/shard_map/pallas_call | solution.py:163
  130.0 8.6 %shard_map.299.refs_1_ = bf16[1024,576]{1,0:T(8,128)(2,1)S(1)} custom-call(s32[4]{0:T(128)S(1)} %pad_add_fusion.refs_1_.refs_0_, bf16[1024,192]{1,0:T(8,128)(2,1)S(1)} %copy-done.40, bf16[3,1024,64]{2,1,0:T(8,128)(2,1)S(1)} %copy-done.32, bf16[3,1024,64]{2,1,0:T(8,128)(2,1)S(1)} %copy-done.37, bf16[192,1024]{1,0:T(8,128)(2,1)S(1)} %copy-done.43, ...), custom_call_target="tpu_custom_call" | custom-call | flops 12000000000 | bytes 1048576 | tf_op jit(solution)/shard_map/pallas_call | solution.py:163
  138.8 7.0 %shard_map.300 = (f32[4,104,768]{2,1,0:T(8,128)S(1)}, bf16[4,112,768]{2,1,0:T(8,128)(2,1)S(1)}, f32[256,768]{1,0:T(8,128)S(1)}, f32[256,768]{1,0:T(8,128)S(1)}, bf16[512,768]{1,0:T(8,128)(2,1)S(1)}) custom-call(s32[4]{0:T(128)S(1)} %pad_add_fusion.refs_1_.refs_0_, bf16[1024,576]{1,0:T(8,128)(2,1)S(1)} %shard_map.299.refs_1_, ...), custom_call_target="tpu_custom_call" | custom-call | flops 10499999744 | bytes 1048576 | tf_op jit(solution)/shard_map/pallas_call | solution.py:163
  146.0 1.8 shard_map.301
  148.2 4.1 %collective-permute-start.33 = (bf16[4,112,768]{2,1,0:T(8,128)(2,1)S(1)}, bf16[4,112,768]{2,1,0:T(8,128)(2,1)S(1)}, u32[]{:S(2)}, u32[]{:S(2)}) collective-permute-start(bf16[4,112,768]{2,1,0:T(8,128)(2,1)S(1)} %get-tuple-element.141), channel_id=1, source_target_pairs={{0,4},{4,0},{8,12},{12,8},{16,20},{20,16},{24,28},{28,24},{1,5},{5... | collective-permute-start | bytes 2064392 | tf_op jit(solution)/shard_map/ppermute | solution.py:44
  155.4 14.8 %collective-permute-done.33.refs_2_ = bf16[4,112,768]{2,1,0:T(8,128)(2,1)S(1)} collective-permute-done((bf16[4,112,768]{2,1,0:T(8,128)(2,1)S(1)}, bf16[4,112,768]{2,1,0:T(8,128)(2,1)S(1)}, u32[]{:S(2)}, u32[]{:S(2)}) %collective-permute-start.33) | collective-permute-done | bytes 688160 | tf_op jit(solution)/shard_map/ppermute | solution.py:44
  173.5 2.6 %collective-permute-start.36 = (bf16[112,768]{1,0:T(8,128)(2,1)S(1)}, bf16[112,768]{1,0:T(8,128)(2,1)S(1)}, u32[]{:S(2)}, u32[]{:S(2)}) collective-permute-start(bf16[112,768]{1,0:T(8,128)(2,1)S(1)} %get-tuple-element.146), channel_id=1, source_target_pairs={{0,24},{4,28},{8,16},{12,20},{16,8},{20,12},{24,0},{28,4},{1,25},{... | collective-permute-start | bytes 516104 | tf_op jit(solution)/shard_map/ppermute | solution.py:49
  177.1 10.7 %collective-permute-done.34.refs_2_ = bf16[112,768]{1,0:T(8,128)(2,1)S(1)} collective-permute-done((bf16[112,768]{1,0:T(8,128)(2,1)S(1)}, bf16[112,768]{1,0:T(8,128)(2,1)S(1)}, u32[]{:S(2)}, u32[]{:S(2)}) %collective-permute-start.34) | collective-permute-done | bytes 172064 | tf_op jit(solution)/shard_map/ppermute | solution.py:49
  189.5 5.8 %collective-permute-done.36.refs_4_ = bf16[112,768]{1,0:T(8,128)(2,1)S(1)} collective-permute-done((bf16[112,768]{1,0:T(8,128)(2,1)S(1)}, bf16[112,768]{1,0:T(8,128)(2,1)S(1)}, u32[]{:S(2)}, u32[]{:S(2)}) %collective-permute-start.36) | collective-permute-done | bytes 172064 | tf_op jit(solution)/shard_map/ppermute | solution.py:49
  195.3 2.4 %reduce-scatter.2.cloned.1.call-done = bf16[1,192,768]{2,1,0:T(8,128)(2,1)} async-done(((bf16[8,192,768]{2,1,0:T(8,128)(2,1)}), bf16[1,192,768]{2,1,0:T(8,128)(2,1)}) %reduce-scatter.2.cloned.1.call-update) | async-done | bytes 294928 | tf_op jit(solution)/shard_map/reduce_scatter | solution.py:40
  198.7 1.8 shard_map.304
  203.1 1.9 shard_map.302
  205.1 2.4 %collective-permute-done.38.refs_3_ = bf16[304,192]{1,0:T(8,128)(2,1)S(1)} collective-permute-done((bf16[304,192]{1,0:T(8,128)(2,1)S(1)}, bf16[304,192]{1,0:T(8,128)(2,1)S(1)}, u32[]{:S(2)}, u32[]{:S(2)}) %collective-permute-start.38) | collective-permute-done | bytes 116768 | tf_op jit(solution)/shard_map/ppermute | solution.py:30
  207.4 3.0 %collective-permute-done.39.refs_4_ = bf16[304,192]{1,0:T(8,128)(2,1)S(1)} collective-permute-done((bf16[304,192]{1,0:T(8,128)(2,1)S(1)}, bf16[304,192]{1,0:T(8,128)(2,1)S(1)}, u32[]{:S(2)}, u32[]{:S(2)}) %collective-permute-start.39) | collective-permute-done | bytes 116768 | tf_op jit(solution)/shard_map/ppermute | solution.py:30
  210.5 2.4 %shard_map.305 = (f32[96,576]{1,0:T(8,128)}, f32[96,768]{1,0:T(8,128)}, f32[384,192]{1,0:T(8,128)S(1)}, f32[96,192]{1,0:T(8,128)}, f32[8,192]{1,0:T(8,128)S(1)}) custom-call(s32[4]{0:T(128)S(1)} %pad_add_fusion.refs_1_.refs_0_, bf16[304,192]{1,0:T(8,128)(2,1)S(1)} %get-tuple-element.147.refs_1_, bf16[304,192]{1,0:T(8,128)(2,1)S(1)} %collective-permute-done.37.refs_2_, ...), custom_call_target="tpu_custom_call" | custom-call | flops 3800000000 | bytes 1048576 | tf_op jit(solution)/shard_map/pallas_call | solution.py:163
  (220 shorter events, 59.6 us)
Async XLA Ops:
  7.2 70.0 %all-gather.2.cloned.1.call-start = ((), (), s32[]{:S(2)}) async-start(), calls=%async_computation.1 | async-start | bytes 2654208 | tf_op jit(solution)/shard_map/all_gather | solution.py:961
  10.4 7.2 %collective-permute-start.4 = (bf16[98,768]{1,0:T(8,128)(2,1)S(1)}, bf16[98,768]{1,0:T(8,128)(2,1)S(1)}, u32[]{:S(2)}, u32[]{:S(2)}) collective-permute-start(bf16[98,768]{1,0:T(8,128)(2,1)S(1)} %pad_maximum_fusion.refs_6_), channel_id=1, source_target_pairs={{8,0},{16,8},{24,16},{28,24},{20,28},{12,20},{4,12},{0,4},{9,1},{1... | collective-permute-start | bytes 451592 | tf_op jit(solution)/shard_map/ppermute | solution.py:73
  13.4 5.6 %collective-permute-start.3 = (bf16[98,768]{1,0:T(8,128)(2,1)S(1)}, bf16[98,768]{1,0:T(8,128)(2,1)S(1)}, u32[]{:S(2)}, u32[]{:S(2)}) collective-permute-start(bf16[98,768]{1,0:T(8,128)(2,1)S(1)} %pad_maximum_fusion.refs_6_), channel_id=1, source_target_pairs={{0,8},{8,16},{16,24},{24,28},{28,20},{20,12},{12,4},{4,0},{1,9},{9... | collective-permute-start | bytes 451592 | tf_op jit(solution)/shard_map/ppermute | solution.py:72
  20.6 177.0 %reduce-scatter.2.cloned.1.call-start = ((), (), s32[]{:S(2)}) async-start(), calls=%async_computation.2 | async-start | bytes 2654208 | tf_op jit(solution)/shard_map/reduce_scatter | solution.py:40
  22.8 18.1 %collective-permute-start = (bf16[256,768]{1,0:T(8,128)(2,1)S(1)}, bf16[256,768]{1,0:T(8,128)(2,1)S(1)}, u32[]{:S(2)}, u32[]{:S(2)}) collective-permute-start(bf16[256,768]{1,0:T(8,128)(2,1)S(1)} %bitcast.36), channel_id=1, source_target_pairs={{0,1},{1,0},{2,3},{3,2},{4,5},{5,4},{6,7},{7,6},{8,9},{9,8},{10,11... | collective-permute-start | bytes 1179656 | tf_op jit(solution)/shard_map/ppermute | solution.py:30
  22.8 18.1 %collective-permute-start.1 = (bf16[256,768]{1,0:T(8,128)(2,1)S(1)}, bf16[256,768]{1,0:T(8,128)(2,1)S(1)}, u32[]{:S(2)}, u32[]{:S(2)}) collective-permute-start(bf16[256,768]{1,0:T(8,128)(2,1)S(1)} %bitcast.37), channel_id=1, source_target_pairs={{0,2},{1,3},{2,0},{3,1},{4,6},{5,7},{6,4},{7,5},{8,10},{9,11},{10,... | collective-permute-start | bytes 1179656 | tf_op jit(solution)/shard_map/ppermute | solution.py:30
  24.3 18.0 %collective-permute-start.2 = (bf16[256,768]{1,0:T(8,128)(2,1)S(1)}, bf16[256,768]{1,0:T(8,128)(2,1)S(1)}, u32[]{:S(2)}, u32[]{:S(2)}) collective-permute-start(bf16[256,768]{1,0:T(8,128)(2,1)S(1)} %bitcast.38), channel_id=1, source_target_pairs={{0,3},{1,2},{2,1},{3,0},{4,7},{5,6},{6,5},{7,4},{8,11},{9,10},{10,... | collective-permute-start | bytes 1179656 | tf_op jit(solution)/shard_map/ppermute | solution.py:30
  26.0 6.8 %collective-permute-start.8 = (bf16[98,768]{1,0:T(8,128)(2,1)S(1)}, bf16[98,768]{1,0:T(8,128)(2,1)S(1)}, u32[]{:S(2)}, u32[]{:S(2)}) collective-permute-start(bf16[98,768]{1,0:T(8,128)(2,1)S(1)} %collective-permute-done.6.refs_10_), channel_id=1, source_target_pairs={{8,0},{16,8},{24,16},{28,24},{20,28},{12,20},{4,12},{0,4},{9,1},{1... | collective-permute-start | bytes 451592 | tf_op jit(solution)/shard_map/ppermute | solution.py:73
  27.6 7.8 %collective-permute-start.7 = (bf16[98,768]{1,0:T(8,128)(2,1)S(1)}, bf16[98,768]{1,0:T(8,128)(2,1)S(1)}, u32[]{:S(2)}, u32[]{:S(2)}) collective-permute-start(bf16[98,768]{1,0:T(8,128)(2,1)S(1)} %collective-permute-done.5.refs_9_), channel_id=1, source_target_pairs={{0,8},{8,16},{16,24},{24,28},{28,20},{20,12},{12,4},{4,0},{1,9},{9... | collective-permute-start | bytes 451592 | tf_op jit(solution)/shard_map/ppermute | solution.py:72
  32.9 8.0 %collective-permute-start.10 = (bf16[50,768]{1,0:T(8,128)(2,1)S(1)}, bf16[50,768]{1,0:T(8,128)(2,1)S(1)}, u32[]{:S(2)}, u32[]{:S(2)}) collective-permute-start(bf16[50,768]{1,0:T(8,128)(2,1)S(1)} %slice.64), channel_id=1, source_target_pairs={{8,0},{16,8},{24,16},{28,24},{20,28},{12,20},{4,12},{0,4},{9,1},{1... | collective-permute-start | bytes 230408 | tf_op jit(solution)/shard_map/ppermute | solution.py:76
  35.4 5.4 %collective-permute-start.9 = (bf16[48,768]{1,0:T(8,128)(2,1)S(1)}, bf16[48,768]{1,0:T(8,128)(2,1)S(1)}, u32[]{:S(2)}, u32[]{:S(2)}) collective-permute-start(bf16[48,768]{1,0:T(8,128)(2,1)S(1)} %slice.63), channel_id=1, source_target_pairs={{0,8},{8,16},{16,24},{24,28},{28,20},{20,12},{12,4},{4,0},{1,9},{9... | collective-permute-start | bytes 221192 | tf_op jit(solution)/shard_map/ppermute | solution.py:76
  45.8 12.7 %collective-permute-start.15 = (bf16[768,192]{1,0:T(8,128)(2,1)S(1)}, bf16[768,192]{1,0:T(8,128)(2,1)S(1)}, u32[]{:S(2)}, u32[]{:S(2)}) collective-permute-start(bf16[768,192]{1,0:T(8,128)(2,1)S(1)} %get-tuple-element.95.refs_8_), channel_id=1, source_target_pairs={{0,2},{1,3},{2,0},{3,1},{4,6},{5,7},{6,4},{7,5},{8,10},{9,11},{10,... | collective-permute-start | bytes 884744 | tf_op jit(solution)/shard_map/ppermute | solution.py:30
  47.4 19.3 %collective-permute-start.14 = (bf16[768,192]{1,0:T(8,128)(2,1)S(1)}, bf16[768,192]{1,0:T(8,128)(2,1)S(1)}, u32[]{:S(2)}, u32[]{:S(2)}) collective-permute-start(bf16[768,192]{1,0:T(8,128)(2,1)S(1)} %get-tuple-element.95.refs_8_), channel_id=1, source_target_pairs={{0,1},{1,0},{2,3},{3,2},{4,5},{5,4},{6,7},{7,6},{8,9},{9,8},{10,11... | collective-permute-start | bytes 884744 | tf_op jit(solution)/shard_map/ppermute | solution.py:30
  58.5 8.2 %collective-permute-start.16 = (bf16[768,192]{1,0:T(8,128)(2,1)S(1)}, bf16[768,192]{1,0:T(8,128)(2,1)S(1)}, u32[]{:S(2)}, u32[]{:S(2)}) collective-permute-start(bf16[768,192]{1,0:T(8,128)(2,1)S(1)} %collective-permute-done.15.refs_10_), channel_id=1, source_target_pairs={{0,1},{1,0},{2,3},{3,2},{4,5},{5,4},{6,7},{7,6},{8,9},{9,8},{10,11... | collective-permute-start | bytes 884744 | tf_op jit(solution)/shard_map/ppermute | solution.py:30
  59.1 6.3 %collective-permute-start.12 = (bf16[256,192]{1,0:T(8,128)(2,1)S(1)}, bf16[256,192]{1,0:T(8,128)(2,1)S(1)}, u32[]{:S(2)}, u32[]{:S(2)}) collective-permute-start(bf16[256,192]{1,0:T(8,128)(2,1)S(1)} %get-tuple-element.90.refs_7_), channel_id=1, source_target_pairs={{0,2},{1,3},{2,0},{3,1},{4,6},{5,7},{6,4},{7,5},{8,10},{9,11},{10,... | collective-permute-start | bytes 294920 | tf_op jit(solution)/shard_map/ppermute | solution.py:30
  59.6 7.1 %collective-permute-start.13 = (bf16[256,192]{1,0:T(8,128)(2,1)S(1)}, bf16[256,192]{1,0:T(8,128)(2,1)S(1)}, u32[]{:S(2)}, u32[]{:S(2)}) collective-permute-start(bf16[256,192]{1,0:T(8,128)(2,1)S(1)} %get-tuple-element.94.refs_8_), channel_id=1, source_target_pairs={{0,3},{1,2},{2,1},{3,0},{4,7},{5,6},{6,5},{7,4},{8,11},{9,10},{10,... | collective-permute-start | bytes 294920 | tf_op jit(solution)/shard_map/ppermute | solution.py:30
  60.6 15.8 %collective-permute-start.18 = (bf16[256,768]{1,0:T(8,128)(2,1)S(1)}, bf16[256,768]{1,0:T(8,128)(2,1)S(1)}, u32[]{:S(2)}, u32[]{:S(2)}) collective-permute-start(bf16[256,768]{1,0:T(8,128)(2,1)S(1)} %bitcast.31), channel_id=1, source_target_pairs={{0,1},{1,0},{2,3},{3,2},{4,5},{5,4},{6,7},{7,6},{8,9},{9,8},{10,11... | collective-permute-start | bytes 1179656 | tf_op jit(solution)/shard_map/ppermute | solution.py:30
  65.4 10.5 %collective-permute-start.21 = (bf16[256,768]{1,0:T(8,128)(2,1)S(1)}, bf16[256,768]{1,0:T(8,128)(2,1)S(1)}, u32[]{:S(2)}, u32[]{:S(2)}) collective-permute-start(bf16[256,768]{1,0:T(8,128)(2,1)S(1)} %bitcast.32), channel_id=1, source_target_pairs={{0,2},{1,3},{2,0},{3,1},{4,6},{5,7},{6,4},{7,5},{8,10},{9,11},{10,... | collective-permute-start | bytes 1179656 | tf_op jit(solution)/shard_map/ppermute | solution.py:30
  75.9 11.6 %collective-permute-start.22 = (bf16[256,768]{1,0:T(8,128)(2,1)S(1)}, bf16[256,768]{1,0:T(8,128)(2,1)}, u32[]{:S(2)}, u32[]{:S(2)}) collective-permute-start(bf16[256,768]{1,0:T(8,128)(2,1)S(1)} %collective-permute-done.21.refs_4_.refs_6_), channel_id=1, source_target_pairs={{0,1},{1,0},{2,3},{3,2},{4,5},{5,4},{6,7},{7,6},{8,9},{9,8},{10,11... | collective-permute-start | bytes 1179656 | tf_op jit(solution)/shard_map/ppermute | solution.py:30
  75.9 11.6 %collective-permute-start.19 = (bf16[256,768]{1,0:T(8,128)(2,1)S(1)}, bf16[256,768]{1,0:T(8,128)(2,1)}, u32[]{:S(2)}, u32[]{:S(2)}) collective-permute-start(bf16[256,768]{1,0:T(8,128)(2,1)S(1)} %get-tuple-element.98.refs_2_.refs_0_), channel_id=1, source_target_pairs={{0,2},{1,3},{2,0},{3,1},{4,6},{5,7},{6,4},{7,5},{8,10},{9,11},{10,... | collective-permute-start | bytes 1179656 | tf_op jit(solution)/shard_map/ppermute | solution.py:30
  95.4 13.9 %collective-permute-start.23 = (bf16[256,768]{1,0:T(8,128)(2,1)}, bf16[256,768]{1,0:T(8,128)(2,1)}, u32[]{:S(2)}, u32[]{:S(2)}) collective-permute-start(bf16[256,768]{1,0:T(8,128)(2,1)} %get-tuple-element.111), channel_id=1, source_target_pairs={{0,1},{1,0},{2,3},{3,2},{4,5},{5,4},{6,7},{7,6},{8,9},{9,8},{10,11... | collective-permute-start | bytes 1179656 | tf_op jit(solution)/shard_map/ppermute | solution.py:30
  97.9 11.5 %collective-permute-start.25 = (bf16[256,768]{1,0:T(8,128)(2,1)}, bf16[256,768]{1,0:T(8,128)(2,1)}, u32[]{:S(2)}, u32[]{:S(2)}) collective-permute-start(bf16[256,768]{1,0:T(8,128)(2,1)} %add_convert_fusion.3), channel_id=1, source_target_pairs={{0,2},{1,3},{2,0},{3,1},{4,6},{5,7},{6,4},{7,5},{8,10},{9,11},{10,... | collective-permute-start | bytes 1179656 | tf_op jit(solution)/shard_map/ppermute | solution.py:30
  113.4 14.7 %collective-permute-start.27 = (bf16[256,768]{1,0:T(8,128)(2,1)S(1)}, bf16[256,768]{1,0:T(8,128)(2,1)S(1)}, u32[]{:S(2)}, u32[]{:S(2)}) collective-permute-start(bf16[256,768]{1,0:T(8,128)(2,1)S(1)} %get-tuple-element.118.refs_6_.refs_9_), channel_id=1, source_target_pairs={{0,2},{1,3},{2,0},{3,1},{4,6},{5,7},{6,4},{7,5},{8,10},{9,11},{10,... | collective-permute-start | bytes 1179656 | tf_op jit(solution)/shard_map/ppermute | solution.py:30
  145.7 6.5 %collective-permute-start.30 = (bf16[512,768]{1,0:T(8,128)(2,1)S(1)}, bf16[512,768]{1,0:T(8,128)(2,1)S(1)}, u32[]{:S(2)}, u32[]{:S(2)}) collective-permute-start(bf16[512,768]{1,0:T(8,128)(2,1)S(1)} %get-tuple-element.131), channel_id=1, source_target_pairs={{0,1},{1,0},{2,3},{3,2},{4,5},{5,4},{6,7},{7,6},{8,9},{9,8},{10,11... | collective-permute-start | bytes 2359304 | tf_op jit(solution)/shard_map/ppermute | solution.py:30
  148.2 22.0 %collective-permute-start.33 = (bf16[4,112,768]{2,1,0:T(8,128)(2,1)S(1)}, bf16[4,112,768]{2,1,0:T(8,128)(2,1)S(1)}, u32[]{:S(2)}, u32[]{:S(2)}) collective-permute-start(bf16[4,112,768]{2,1,0:T(8,128)(2,1)S(1)} %get-tuple-element.141), channel_id=1, source_target_pairs={{0,4},{4,0},{8,12},{12,8},{16,20},{20,16},{24,28},{28,24},{1,5},{5... | collective-permute-start | bytes 2064392 | tf_op jit(solution)/shard_map/ppermute | solution.py:44
  153.2 22.9 %collective-permute-start.31 = (bf16[256,768]{1,0:T(8,128)(2,1)S(1)}, bf16[256,768]{1,0:T(8,128)(2,1)S(1)}, u32[]{:S(2)}, u32[]{:S(2)}) collective-permute-start(bf16[256,768]{1,0:T(8,128)(2,1)S(1)} %add_convert_fusion.2), channel_id=1, source_target_pairs={{0,2},{1,3},{2,0},{3,1},{4,6},{5,7},{6,4},{7,5},{8,10},{9,11},{10,... | collective-permute-start | bytes 1179656 | tf_op jit(solution)/shard_map/ppermute | solution.py:30
  154.1 49.0 %collective-permute-start.32 = (bf16[256,768]{1,0:T(8,128)(2,1)}, bf16[256,768]{1,0:T(8,128)(2,1)S(1)}, u32[]{:S(2)}, u32[]{:S(2)}) collective-permute-start(bf16[256,768]{1,0:T(8,128)(2,1)} %add_convert_fusion.1), channel_id=1, source_target_pairs={{0,2},{1,3},{2,0},{3,1},{4,6},{5,7},{6,4},{7,5},{8,10},{9,11},{10,... | collective-permute-start | bytes 1179656 | tf_op jit(solution)/shard_map/ppermute | solution.py:30
  171.7 16.1 %collective-permute-start.34 = (bf16[112,768]{1,0:T(8,128)(2,1)S(1)}, bf16[112,768]{1,0:T(8,128)(2,1)S(1)}, u32[]{:S(2)}, u32[]{:S(2)}) collective-permute-start(bf16[112,768]{1,0:T(8,128)(2,1)S(1)} %get-tuple-element.144), channel_id=1, source_target_pairs={{0,8},{4,12},{8,0},{12,4},{16,24},{20,28},{24,16},{28,20},{1,9},{5... | collective-permute-start | bytes 516104 | tf_op jit(solution)/shard_map/ppermute | solution.py:49
  172.7 16.8 %collective-permute-start.35 = (bf16[112,768]{1,0:T(8,128)(2,1)S(1)}, bf16[112,768]{1,0:T(8,128)(2,1)S(1)}, u32[]{:S(2)}, u32[]{:S(2)}) collective-permute-start(bf16[112,768]{1,0:T(8,128)(2,1)S(1)} %get-tuple-element.145), channel_id=1, source_target_pairs={{0,16},{4,20},{8,24},{12,28},{16,0},{20,4},{24,8},{28,12},{1,17},{... | collective-permute-start | bytes 516104 | tf_op jit(solution)/shard_map/ppermute | solution.py:49
  173.5 21.8 %collective-permute-start.36 = (bf16[112,768]{1,0:T(8,128)(2,1)S(1)}, bf16[112,768]{1,0:T(8,128)(2,1)S(1)}, u32[]{:S(2)}, u32[]{:S(2)}) collective-permute-start(bf16[112,768]{1,0:T(8,128)(2,1)S(1)} %get-tuple-element.146), channel_id=1, source_target_pairs={{0,24},{4,28},{8,16},{12,20},{16,8},{20,12},{24,0},{28,4},{1,25},{... | collective-permute-start | bytes 516104 | tf_op jit(solution)/shard_map/ppermute | solution.py:49
  200.6 6.8 %collective-permute-start.38 = (bf16[304,192]{1,0:T(8,128)(2,1)S(1)}, bf16[304,192]{1,0:T(8,128)(2,1)S(1)}, u32[]{:S(2)}, u32[]{:S(2)}) collective-permute-start(bf16[304,192]{1,0:T(8,128)(2,1)S(1)} %get-tuple-element.149), channel_id=1, source_target_pairs={{0,2},{1,3},{2,0},{3,1},{4,6},{5,7},{6,4},{7,5},{8,10},{9,11},{10,... | collective-permute-start | bytes 350216 | tf_op jit(solution)/shard_map/ppermute | solution.py:30
  202.2 8.3 %collective-permute-start.39 = (bf16[304,192]{1,0:T(8,128)(2,1)S(1)}, bf16[304,192]{1,0:T(8,128)(2,1)S(1)}, u32[]{:S(2)}, u32[]{:S(2)}) collective-permute-start(bf16[304,192]{1,0:T(8,128)(2,1)S(1)} %get-tuple-element.150), channel_id=1, source_target_pairs={{0,3},{1,2},{2,1},{3,0},{4,7},{5,6},{6,5},{7,4},{8,11},{9,10},{10,... | collective-permute-start | bytes 350216 | tf_op jit(solution)/shard_map/ppermute | solution.py:30
  (70 other events, 408.0 us)
Sparse Core Ops, SparseCore 0:
  20.8 53.8 all-gather.1
  113.5 84.1 reduce-scatter.1
